TPU v7x, 256 devices: a whole 4x4x8 slice. The times are simulated.
256 devices in a mesh: replica: 2 (over core), lists: 128 (over z, x, y).
Axes of the slice: x: 4, y: 4, z: 8, core: 2. Of those that a mesh axis runs over, the one named last changes fastest.
Arguments:
- inserts: bfloat16 [32768, 1024], P(('replica', 'lists')), may hold values from -6 to 6
- list_ids: int32 [32768], P(('replica', 'lists')), may hold values from 0 to 131071, as said below
- centroids: bfloat16 [131072, 1024], P('lists'), may hold values from -6 to 6
- prior_counts: int32 [131072], P('lists'), may hold values from 1 to 16
- rotation: bfloat16 [1024, 1024], replicated, may hold values from -0.1875 to 0.1875
Outputs:
- new_centroids: bfloat16 [131072, 1024], P('lists')
- rotated: bfloat16 [32768, 1024], P(('replica', 'lists'))
Inputs may be any that keep to these rules, and one draw needn't show every extreme that they name: `list_ids`: list k belongs to index k // 1024 of lists. In each aligned block of 128 inserts (the rows of one device) at most 4 inserts name lists of one index; in every draw one index receives exactly 4 from every block, every other index at most 1.
All inputs are finite; a program needn't handle non-finite values.
Results may differ from a plain program's by a relative error of at most 0.0055.
Values may be sent and summed in bfloat16 or wider, within the bound.
A program may use at most 128 MiB of HBM per device.

v0:
```python
import jax
import jax.numpy as jnp
from jax import lax
from jax.sharding import PartitionSpec as P


def refresh(old_rows, prior_rows, sum_rows, count_rows):
    old_float = old_rows.astype(jnp.float32)
    denominator = prior_rows.astype(jnp.float32) + count_rows
    updated = old_float + (sum_rows - count_rows[:, None] * old_float) / denominator[:, None]
    return updated.astype(jnp.bfloat16)


def accumulate_slots(rows_flat, ids_flat, lists_here, block_size):
    width = rows_flat.shape[1]
    list_range = jnp.arange(lists_here, dtype=jnp.int32)
    sums = jnp.zeros((lists_here, width), jnp.float32)
    counts = jnp.zeros((lists_here,), jnp.float32)
    for block in range(rows_flat.shape[0] // block_size):
        block_ids = ids_flat[block * block_size : (block + 1) * block_size]
        block_rows = rows_flat[block * block_size : (block + 1) * block_size]
        matches = list_range[:, None] == block_ids[None, :]
        sums = sums + jnp.dot(
            matches.astype(jnp.bfloat16), block_rows, preferred_element_type=jnp.float32
        )
        counts = counts + jnp.sum(matches.astype(jnp.float32), axis=1)
    return (sums, counts)


def per_device(inserts, list_ids, centroids, prior_counts, rotation):
    owners = lax.axis_size("lists")
    lists_here = centroids.shape[0]
    row_count = inserts.shape[0]
    width = inserts.shape[1]
    slot_size = 4 * row_count // owners
    owner_of = list_ids // lists_here
    local_id = list_ids - owner_of * lists_here
    owner_hits = (owner_of[:, None] == jnp.arange(owners, dtype=jnp.int32)[None, :]).astype(
        jnp.int32
    )
    slot_rank = jnp.sum((jnp.cumsum(owner_hits, axis=0) - 1) * owner_hits, axis=1)
    position = owner_of * slot_size + slot_rank
    source = (
        jnp.zeros((owners * slot_size,), jnp.int32)
        .at[position]
        .set(jnp.arange(row_count, dtype=jnp.int32) + 1)
    )
    filled = source > 0
    source_row = jnp.maximum(source - 1, 0)
    send_rows = jnp.where(
        filled[:, None], inserts[source_row], jnp.zeros((), jnp.bfloat16)
    ).reshape(owners, slot_size, width)
    send_ids = jnp.where(filled, local_id[source_row], -1).reshape(owners, slot_size)
    got_rows, got_ids = (
        lax.all_to_all(send_rows, "lists", split_axis=0, concat_axis=0, tiled=True),
        lax.all_to_all(send_ids, "lists", split_axis=0, concat_axis=0, tiled=True),
    )
    rows_flat = got_rows.reshape(owners * slot_size, width)
    ids_flat = got_ids.reshape(owners * slot_size)
    sums, counts = accumulate_slots(rows_flat, ids_flat, lists_here, row_count)
    total_sums, total_counts = lax.psum((sums, counts), "replica")
    new_centroids = refresh(centroids, prior_counts, total_sums, total_counts)
    safe_ids = jnp.maximum(ids_flat, 0)
    picked = new_centroids[safe_ids].astype(jnp.float32)
    residual_rows = (rows_flat.astype(jnp.float32) - picked).astype(jnp.bfloat16)
    rotated_slots = jnp.dot(residual_rows, rotation, preferred_element_type=jnp.float32).astype(
        jnp.bfloat16
    )
    returned = lax.all_to_all(
        rotated_slots.reshape(owners, slot_size, width),
        "lists",
        split_axis=0,
        concat_axis=0,
        tiled=True,
    )
    rotated = returned.reshape(owners * slot_size, width)[position]
    return (new_centroids, rotated)


def solution(mesh):
    placed = (
        P(("replica", "lists"), None),
        P(("replica", "lists")),
        P("lists", None),
        P("lists"),
        P(),
    )
    return jax.shard_map(
        per_device,
        mesh=mesh,
        in_specs=placed,
        out_specs=(P("lists", None), P(("replica", "lists"), None)),
        check_vma=False,
    )
```

profile of v0, /device:TPU:1, one launch (start us, length us, event | category | flops | bytes accessed | tf_op | source)
XLA Modules:
  0.0 194.3 jit_solution(17551665711672246747)
XLA Ops:
  7.2 0.0 copy-start
  7.2 0.0 copy-start.1
  7.2 0.8 multiply_subtract_fusion
  8.0 0.1 fusion.10
  8.1 0.2 reduce_window_sum.11
  8.3 0.2 select_reduce_fusion
  8.5 1.0 scatter_custom_fusion
  9.5 3.3 %gather_fusion = s32[512]{0:T(512)S(1)} fusion(s32[128]{0:T(128)S(1)} %get-tuple-element.8, s32[1024]{0:T(1024)S(1)} %pad_clamp_fusion.2), kind=kCustom, calls=%fused_computation | custom fusion | bytes 6144 | tf_op jit(solution)/shard_map/gather | solution.py:53
  12.8 0.7 all_to_all.12
  13.6 16.3 %all-to-all-start = ((s32[128,1,4]{2,1,0:T(1,128)}), s32[128,1,4]{2,1,0:T(1,128)S(1)}, u32[]{:S(2)}, u32[]{:S(2)}) async-start(s32[128,1,4]{2,1,0:T(1,128)} %bitcast), calls=%async_computation | async-start | bytes 131072 | tf_op jit(solution)/shard_map/all_to_all | solution.py:56
  29.9 0.1 broadcast_in_dim.22
  30.1 0.0 copy-done.1
  30.1 2.1 %gather_fusion.1 = bf16[512,1024]{1,0:T(8,128)(2,1)S(1)} fusion(bf16[128,1024]{1,0:T(8,128)(2,1)S(1)} %copy-done.1, s32[1024]{0:T(1024)S(1)} %pad_clamp_fusion.2), kind=kCustom, calls=%fused_computation.1 | custom fusion | bytes 2099200 | tf_op jit(solution)/shard_map/gather | solution.py:51
  32.1 1.2 gather.16
  33.3 2.7 %broadcast_select_fusion = bf16[128,4,1024]{2,1,0:T(4,128)(2,1)} fusion(bf16[128,4,1024]{2,1,0:T(4,128)(2,1)} %gather.16, pred[128,4]{1,0:T(8,128)(4,1)S(1)} %broadcast_in_dim.22), kind=kLoop, calls=%fused_computation.13 | loop fusion | flops 524288 | bytes 2097664 | tf_op jit(solution)/shard_map/jit(_where)/select_n | solution.py:50
  36.1 4.5 %all-to-all-done = s32[128,1,4]{2,1,0:T(1,128)S(1)} async-done(((s32[128,1,4]{2,1,0:T(1,128)}), s32[128,1,4]{2,1,0:T(1,128)S(1)}, u32[]{:S(2)}, u32[]{:S(2)}) %all-to-all-start) | async-done | bytes 2080 | tf_op jit(solution)/shard_map/all_to_all | solution.py:56
  40.6 8.7 %all-to-all-start.1 = ((bf16[128,4,1024]{2,1,0:T(4,128)(2,1)}), bf16[128,4,1024]{2,1,0:T(4,128)(2,1)S(1)}, u32[]{:S(2)}, u32[]{:S(2)}) async-start(bf16[128,4,1024]{2,1,0:T(4,128)(2,1)} %broadcast_select_fusion), calls=%async_computation.1 | async-start | bytes 2097152 | tf_op jit(solution)/shard_map/all_to_all | solution.py:55
  49.3 0.0 all-reduce.2.cloned.1.call-start
  49.3 0.2 slice_reduce_fusion
  49.5 0.1 eq.81
  49.6 0.1 eq.77
  49.7 0.1 eq.85
  49.8 0.1 eq.89
  49.9 27.4 %all-to-all-done.1 = bf16[128,4,1024]{2,1,0:T(4,128)(2,1)S(1)} async-done(((bf16[128,4,1024]{2,1,0:T(4,128)(2,1)}), bf16[128,4,1024]{2,1,0:T(4,128)(2,1)S(1)}, u32[]{:S(2)}, u32[]{:S(2)}) %all-to-all-start.1) | async-done | bytes 1048608 | tf_op jit(solution)/shard_map/all_to_all | solution.py:55
  77.3 1.2 fusion.13
  78.5 1.7 slice.49
  80.2 1.7 slice.46
  81.9 0.8 slice.52
  82.7 1.0 slice.55
  83.7 0.0 copy-start.2
  83.7 0.0 copy-start.3
  83.7 1.7 fusion.4
  85.4 0.0 copy-done.2
  85.5 0.7 fusion.5
  86.1 0.0 copy-done.3
  86.2 0.7 fusion.3
  86.9 2.7 %add_add_fusion = f32[1024,1024]{1,0:T(8,128)} fusion(f32[1024,1024]{1,0:T(8,128)S(1)} %fusion.3, f32[1024,1024]{1,0:T(8,128)S(1)} %fusion.5, f32[1024,1024]{1,0:T(8,128)S(1)} %fusion.4, bf16[128,1024]{1,0:T(8,128)(2,1)S(1)} %slice.55, s32[128]{0:T(128)S(1)} %eq.89), kind=kOutput, calls=%fused_computation.9 | convolution fusion | flops 271712256 | bytes 17039872 | tf_op jit(solution)/shard_map/dot_general | solution.py:23
  89.6 0.0 copy-start.4
  89.6 0.0 all-reduce.2.cloned.1.call-update
  89.6 0.2 maximum_reduce_fusion
  89.8 0.1 reshape.87
  89.9 0.1 convert_reduce_fusion
  90.0 0.1 convert_reduce_fusion.1
  90.2 0.1 convert_reduce_fusion.2
  90.3 0.1 convert_reduce_fusion.3
  90.5 6.3 %psum.15 = f32[1024]{0:T(1024)S(1)} all-reduce(f32[1024]{0:T(1024)S(1)} %add_add_fusion.1), channel_id=1, replica_groups=mesh['replica'=2,'lists'=128] {'replica'}, use_global_device_ids=true, to_apply=%region_8.9 | all-reduce | flops 1024 | bytes 8192 | tf_op jit(solution)/shard_map/psum | solution.py:61
  96.8 0.0 copy-done.4
  96.8 1.5 reshape.68
  98.3 28.1 %all-reduce.2.cloned.1.call-done = f32[1024,1024]{1,0:T(8,128)} async-done(((f32[1024,1024]{1,0:T(8,128)}), f32[1024,1024]{1,0:T(8,128)}) %all-reduce.2.cloned.1.call-update) | async-done | bytes 4194320 | tf_op jit(solution)/shard_map/psum | solution.py:61
  126.4 4.3 %fusion.2 = bf16[1024,1024]{1,0:T(8,128)(2,1)} fusion(f32[1024,1024]{1,0:T(8,128)} %all-reduce.2.cloned.1.call-done, bf16[1024,1024]{1,0:T(8,128)(2,1)} %param.7, f32[1024]{0:T(1024)S(1)} %convert_add_fusion.1, f32[1024]{0:T(1024)S(1)} %psum.15), kind=kLoop, calls=%fused_computation.10 | loop fusion | flops 6291456 | bytes 8396800 | tf_op jit(solution)/shard_map/convert_element_type | solution.py:11
  130.7 4.6 %gather_fusion.2 = bf16[512,1024]{1,0:T(8,128)(2,1)S(1)} fusion(bf16[1024,1024]{1,0:T(8,128)(2,1)} %fusion.2, s32[1024]{0:T(1024)S(1)} %pad_clamp_fusion.1), kind=kCustom, calls=%fused_computation.2 | custom fusion | bytes 2099200 | tf_op jit(solution)/shard_map/gather | solution.py:64
  135.3 0.0 copy-done
  135.3 3.8 %convolution_convert_fusion = bf16[512,1024]{1,0:T(8,128)(2,1)} fusion(bf16[1024,1024]{1,0:T(8,128)(2,1)S(1)} %copy-done, f32[512,1024]{1,0:T(8,128)} %reshape.68, bf16[512,1024]{1,0:T(8,128)(2,1)S(1)} %gather_fusion.2), kind=kOutput, calls=%fused_computation.12 | convolution fusion | flops 1075838976 | bytes 6291456 | tf_op jit(solution)/shard_map/dot_general | solution.py:66
  139.2 2.3 %reshape.66 = bf16[128,4,1024]{2,1,0:T(4,128)(2,1)} reshape(bf16[512,1024]{1,0:T(8,128)(2,1)} %convolution_convert_fusion) | data formatting | bytes 2097152 | tf_op jit(solution)/shard_map/reshape | solution.py:70
  141.5 14.1 %all-to-all-start.2 = ((bf16[128,4,1024]{2,1,0:T(4,128)(2,1)}), bf16[128,4,1024]{2,1,0:T(4,128)(2,1)}, u32[]{:S(2)}, u32[]{:S(2)}) async-start(bf16[128,4,1024]{2,1,0:T(4,128)(2,1)} %reshape.66), calls=%async_computation.2 | async-start | bytes 2097152 | tf_op jit(solution)/shard_map/all_to_all | solution.py:69
  155.6 29.0 %all-to-all-done.2 = bf16[128,4,1024]{2,1,0:T(4,128)(2,1)} async-done(((bf16[128,4,1024]{2,1,0:T(4,128)(2,1)}), bf16[128,4,1024]{2,1,0:T(4,128)(2,1)}, u32[]{:S(2)}, u32[]{:S(2)}) %all-to-all-start.2) | async-done | bytes 1048608 | tf_op jit(solution)/shard_map/all_to_all | solution.py:69
  184.5 1.3 reshape.67
  185.9 1.6 gather_fusion.3
  (8 shorter events, 0.0 us)
Async XLA Ops:
  7.2 128.2 %copy-start = (bf16[1024,1024]{1,0:T(8,128)(2,1)S(1)}, bf16[1024,1024]{1,0:T(8,128)(2,1)}, u32[]{:S(2)}) copy-start(bf16[1024,1024]{1,0:T(8,128)(2,1)} %param.9) | copy-start | bytes 6291460
  7.2 22.9 %copy-start.1 = (bf16[128,1024]{1,0:T(8,128)(2,1)S(1)}, bf16[128,1024]{1,0:T(8,128)(2,1)}, u32[]{:S(2)}) copy-start(bf16[128,1024]{1,0:T(8,128)(2,1)} %param.5) | copy-start | bytes 786436
  13.6 27.0 %all-to-all-start = ((s32[128,1,4]{2,1,0:T(1,128)}), s32[128,1,4]{2,1,0:T(1,128)S(1)}, u32[]{:S(2)}, u32[]{:S(2)}) async-start(s32[128,1,4]{2,1,0:T(1,128)} %bitcast), calls=%async_computation | async-start | bytes 131072 | tf_op jit(solution)/shard_map/all_to_all | solution.py:56
  40.6 36.7 %all-to-all-start.1 = ((bf16[128,4,1024]{2,1,0:T(4,128)(2,1)}), bf16[128,4,1024]{2,1,0:T(4,128)(2,1)S(1)}, u32[]{:S(2)}, u32[]{:S(2)}) async-start(bf16[128,4,1024]{2,1,0:T(4,128)(2,1)} %broadcast_select_fusion), calls=%async_computation.1 | async-start | bytes 2097152 | tf_op jit(solution)/shard_map/all_to_all | solution.py:55
  49.3 77.1 %all-reduce.2.cloned.1.call-start = ((), (), s32[]{:S(2)}) async-start(), calls=%async_computation.3 | async-start | bytes 8388608 | tf_op jit(solution)/shard_map/psum | solution.py:61
  83.7 1.7 copy-start.2
  83.7 2.4 %copy-start.3 = (bf16[128,1024]{1,0:T(8,128)(2,1)S(1)}, bf16[128,1024]{1,0:T(8,128)(2,1)}, u32[]{:S(2)}) copy-start(bf16[128,1024]{1,0:T(8,128)(2,1)} %slice.52) | copy-start | bytes 786436
  89.6 7.3 %copy-start.4 = (s32[1024]{0:T(1024)S(1)}, s32[1024]{0:T(1024)}, u32[]{:S(2)}) copy-start(s32[1024]{0:T(1024)} %param.8) | copy-start | bytes 12292
  141.5 43.1 %all-to-all-start.2 = ((bf16[128,4,1024]{2,1,0:T(4,128)(2,1)}), bf16[128,4,1024]{2,1,0:T(4,128)(2,1)}, u32[]{:S(2)}, u32[]{:S(2)}) async-start(bf16[128,4,1024]{2,1,0:T(4,128)(2,1)} %reshape.66), calls=%async_computation.2 | async-start | bytes 2097152 | tf_op jit(solution)/shard_map/all_to_all | solution.py:69
Sparse Core Ops, SparseCore 0:
  89.7 36.6 all-reduce.1
where the time goes:
time: 195 us; the launch traced here: 194 us
  waiting for transfers between devices  89 us (46%)
  starting transfers between devices  39.1 us (20%)
  local copies, waits for them, and re-layouts  26.8 us (14%)
  between operations  14.3 us (7%)
  matrix products  9.61 us (5%)
  other arithmetic  9.14 us (5%)
  blocking collectives  6.31 us (3%)
    all_to_all x1, waiting for transfers between devices, per_device(): lax.all_to_all(rotated_slots.reshape(owners, slot_size, width), 'lists',...  29 us
    psum x1, waiting for transfers between devices, per_device(): total_sums, total_counts = lax.psum((sums, counts), 'replica')  28.1 us
    all_to_all x1, waiting for transfers between devices, per_device(): lax.all_to_all(send_rows, 'lists', split_axis=0, concat_axis=0, tiled=True)  27.4 us
    all_to_all x1, starting transfers between devices, per_device(): lax.all_to_all(send_ids, 'lists', split_axis=0, concat_axis=0, tiled=True)  16.3 us
    all_to_all x1, starting transfers between devices, per_device(): lax.all_to_all(rotated_slots.reshape(owners, slot_size, width), 'lists',...  14.1 us
    all_to_all x1, starting transfers between devices, per_device(): lax.all_to_all(send_rows, 'lists', split_axis=0, concat_axis=0, tiled=True)  8.68 us
    slice x5, local copies, waits for them, and re-layouts, accumulate_slots(): block_rows = rows_flat[block * block_size:(block + 1) * block_size]  6.39 us
    psum x1, blocking collectives, per_device(): total_sums, total_counts = lax.psum((sums, counts), 'replica')  6.31 us
  transfers between devices with their start and end apart: 4, of which 4 were waited for; matrix products, arithmetic and copies ran while one was open for 5% of the time, Pallas kernels for 0%

commit v1 on v0

v1 whole, which is shorter than its diff:
```python
import jax
import jax.numpy as jnp
from jax import lax
from jax.experimental import pallas as pl
from jax.experimental.pallas import tpu as pltpu
from jax.sharding import PartitionSpec as P

MESH = pl.DeviceIdType.MESH
BF = jnp.bfloat16
F32 = jnp.float32
I32 = jnp.int32
STAGES = 20


def mm(a, b):
    return jnp.dot(a, b, preferred_element_type=F32)


def iota(shape, dim):
    return lax.broadcasted_iota(I32, shape, dim)


def onehot(mask):
    return jnp.where(mask, 1.0, 0.0).astype(BF)


def owner_at(zz, gg):
    return (zz << 4) + ((gg & 3) << 2) + (gg >> 2)


def wait_bytes(ref, sem):
    pltpu.make_async_copy(ref, ref, sem).wait()


def kernel(
    ids_ref, x_ref, prior_ref, cent_hbm, rot_hbm, newc_hbm, out_ref,
    sbuf, r1, bbuf, rb1, a2, ra2, b2, rb2, hot_a, hot_b, idb,
    w, wt, cnt, rinv, cvm, rvm, nvm, rowsb,
    ga, gb, gha, ghb, rga, rgb, rha, rhb, fa, fb, rfa, rfb,
    h2a, h2b, rh2a, rh2b, ht, rht, perm, send, recv, local,
):
    c = lax.axis_index("replica")
    li = lax.axis_index("lists")
    z = li // 16
    x = (li // 4) % 4
    y = li % 4
    zc = z * 2 + c
    g = y * 4 + x

    def dev(zc_to, g_to):
        return (zc_to % 2, (zc_to // 2) * 16 + (g_to % 4) * 4 + g_to // 4)

    def start(stage, src, dst, zc_to, g_to):
        pltpu.make_async_remote_copy(
            src_ref=src, dst_ref=dst, send_sem=send.at[stage], recv_sem=recv.at[stage],
            device_id=dev(zc_to, g_to), device_id_type=MESH,
        ).start()

    def along_zc(stage, src, dst):
        @pl.loop(1, 16)
        def _(step):
            to = (zc + step) % 16
            start(stage, src.at[to], dst.at[zc], to, g)

    def along_g(stage, src, dst):
        @pl.loop(1, 16)
        def _(step):
            to = (g + step) % 16
            start(stage, src.at[to], dst.at[g], zc, to)

    barrier = pltpu.get_barrier_semaphore()

    @pl.loop(1, 16)
    def _(step):
        pl.semaphore_signal(barrier, 1, device_id=dev((zc + step) % 16, g), device_id_type=MESH)
        pl.semaphore_signal(barrier, 1, device_id=dev(zc, (g + step) % 16), device_id_type=MESH)

    half = pl.ds(pl.multiple_of(c * 512, 512), 512)
    cent_copy = pltpu.make_async_copy(cent_hbm.at[:, half], cvm, local.at[0])
    rot_copy = pltpu.make_async_copy(rot_hbm, rvm, local.at[1])
    cent_copy.start()
    rot_copy.start()

    ids = ids_ref[...]
    owner_row = ids >> 10
    eye = iota((128, 128), 0) == iota((128, 128), 1)
    owner_col = jnp.sum(jnp.where(eye, owner_row, 0), axis=1, keepdims=True)
    same = jnp.where(owner_col == owner_row, 1.0, 0.0)
    earlier = jnp.where(iota((128, 128), 0) < iota((128, 128), 1), same, 0.0)
    later = jnp.where(iota((128, 128), 1) < iota((128, 128), 0), same, 0.0)
    hot_row = jnp.sum(same, axis=0, keepdims=True) > 1.5
    hot_col = jnp.sum(same, axis=1, keepdims=True) > 1.5
    slot_row = jnp.where(hot_row, jnp.sum(earlier, axis=0, keepdims=True), 4.0)
    slot_col = jnp.where(hot_col, jnp.sum(later, axis=1, keepdims=True), 4.0)

    r128 = iota((128, 128), 0)
    cold_owner_row = jnp.where(hot_row, -1, owner_row)
    pick = onehot(owner_at(r128 >> 4, r128 & 15) == cold_owner_row)
    for cc in range(2):
        block = mm(pick, x_ref[:, cc * 512 : cc * 512 + 256]).astype(BF)
        for t in range(2):
            sbuf[:, cc, t * 16 : t * 16 + 16, :] = block[:, t * 128 : t * 128 + 128].reshape(8, 16, 128)
    tile_row = iota((16, 128), 0)
    for cc in range(2):
        tile = jnp.zeros((16, 128), F32)
        for j in range(4):
            match = (tile_row >> 2 == j) & ((tile_row & 3).astype(F32) == slot_row)
            low = cc * 512 + j * 128
            tile = tile + mm(onehot(match), x_ref[:, low : low + 128])
        sbuf[:, cc, 32:48, :] = jnp.broadcast_to(tile.astype(BF)[None], (8, 16, 128))
    info = jnp.where(tile_row == 0, owner_row, 0)
    info = jnp.where(tile_row == 1, (ids & 1023) >> 5, info)
    info = jnp.where(tile_row == 2, ids & 31, info).astype(F32)
    info = jnp.where(tile_row == 3, slot_row, info).astype(BF)
    for cc in range(2):
        sbuf[:, cc, 48:64, :] = jnp.broadcast_to(info[None], (8, 16, 128))

    r256 = iota((256, 128), 0)
    hit = owner_at((r256 & 15) >> 1, r256 >> 4) == cold_owner_row
    part_b = mm(onehot(hit & ((r256 & 1) == 0)), x_ref[:, 256:512])
    part_b = part_b + mm(onehot(hit & ((r256 & 1) == 1)), x_ref[:, 768:1024])
    bbuf[...] = part_b.astype(BF).reshape(16, 16, 256)

    p0, p1 = iota((256, 256), 0), iota((256, 256), 1)
    perm[...] = onehot((p0 >> 4 == p1 & 15) & (p0 & 15 == p1 >> 4))

    def swap(rows):
        return mm(perm[...], rows).astype(BF)

    sflat = sbuf.at[z, c]
    r1[zc] = sflat[...]
    rb1[g] = bbuf[g]
    pl.semaphore_wait(barrier, 30)

    @pl.loop(1, 16)
    def _(step):
        to = (zc + step) % 16
        start(0, sbuf.at[to // 2, to % 2], r1.at[zc], to, g)

    along_g(1, bbuf, rb1)

    ones = jnp.ones((128, 128), BF)
    for a in range(8):
        diag = jnp.where(eye, prior_ref[a : a + 1, :].astype(F32), 0.0).astype(BF)
        rinv[a * 128 : a * 128 + 128, :] = mm(diag, ones)

    wait_bytes(r1.at[pl.ds(0, 15)], recv.at[0])
    hot = swap(r1[:, 32:48, :].reshape(256, 128)).reshape(4, 4, 16, 128)
    hot_a[:, y, x, :, 0:128] = hot[0]
    hot_a[:, y, x, :, 128:256] = hot[1]
    hot_b[:, y, x, :, 0:128] = hot[2]
    hot_b[:, y, x, :, 128:256] = hot[3]
    got = mm(perm[...], r1[:, 48:64, :].reshape(256, 128)).astype(I32)
    idb[y, x] = (got[48:64] << 17) + (got[0:16] << 10) + (got[16:32] << 5) + got[32:48]
    for step in range(1, 4):
        to = y * 4 + (x + step) % 4
        start(4, hot_a.at[:, y, x], hot_a.at[:, y, x], zc, to)
        start(8, idb.at[y, x], idb.at[y, x], zc, to)
        start(6, hot_b.at[:, y, x], hot_b.at[:, y, x], zc, ((y + step) % 4) * 4 + x)
    for t in range(2):
        moved = swap(r1[:, t * 16 : t * 16 + 16, :].reshape(256, 128))
        a2[:, :, t * 128 : t * 128 + 128] = moved.reshape(16, 16, 128)
    ra2[g] = a2[g]
    along_g(2, a2, ra2)

    wait_bytes(rb1.at[pl.ds(0, 15)], recv.at[1])
    b2[...] = swap(rb1[...].reshape(256, 256)).reshape(16, 16, 256)
    rb2[zc] = b2[zc]
    along_zc(3, b2, rb2)

    wait_bytes(hot_a.at[:, 0, pl.ds(0, 3)], recv.at[4])
    wait_bytes(idb.at[0, pl.ds(0, 3)], recv.at[8])
    wait_bytes(hot_b.at[:, 0, pl.ds(0, 3)], recv.at[6])
    for step in range(1, 4):
        to = ((y + step) % 4) * 4 + x
        start(9, idb.at[y], idb.at[y], zc, to)
        start(5, hot_a.at[:, y], hot_a.at[:, y], zc, to)
        start(7, hot_b.at[:, :, x], hot_b.at[:, :, x], zc, y * 4 + (x + step) % 4)

    wait_bytes(idb.at[pl.ds(0, 3)], recv.at[9])
    code = idb[...].reshape(256, 128)
    mine = ((code >> 10) & 127) == li
    slot = code >> 17
    number = (code & 1023) + 1
    ones8 = jnp.ones((8, 256), BF)
    ones256 = jnp.ones((256, 128), BF)
    for block, s in enumerate((4, 0, 1, 2, 3)):
        here = mine & (slot == s)
        top = jnp.where(here, number & 2016, 0).astype(F32).astype(BF)
        low = jnp.where(here, number & 31, 0).astype(F32).astype(BF)
        both = jnp.concatenate([top, low], axis=1)
        lanes = lax.dot_general(ones8, both, (((1,), (1,)), ((), ())), preferred_element_type=F32)
        lanes = lanes.astype(I32)[0:1, :] - 1
        rows = mm(both, ones256).astype(I32) - 1
        for a in range(8):
            w[a * 128 : a * 128 + 128, block * 256 : block * 256 + 256] = onehot(
                iota((128, 256), 0) + a * 128 == lanes
            )
            wt[block * 256 : block * 256 + 256, a * 128 : a * 128 + 128] = onehot(
                iota((256, 128), 1) + a * 128 == rows
            )
    for a in range(4):
        lists = slice(a * 256, a * 256 + 256)
        total = mm(w[lists, :], jnp.ones((1280, 128), BF))
        cnt[lists, :] = total
        rinv[lists, :] = 1.0 / (rinv[lists, :] + total)

    def refresh(part, cold, hot_rows):
        for a in range(4):
            lists = slice(a * 256, a * 256 + 256)
            cols = slice(part * 256, part * 256 + 256)
            sums = mm(w[lists, 0:256], cold) + mm(w[lists, 256:1280], hot_rows)
            old = cvm[lists, cols].astype(F32)
            count = jnp.concatenate([cnt[lists, :]] * 2, axis=1)
            scale = jnp.concatenate([rinv[lists, :]] * 2, axis=1)
            nvm[lists, cols] = (old + (sums - count * old) * scale).astype(BF)
        return nvm[:, part * 256 : part * 256 + 256]

    cent_copy.wait()
    wait_bytes(ra2.at[pl.ds(0, 15)], recv.at[2])
    wait_bytes(hot_a.at[:, pl.ds(0, 3)], recv.at[5])
    new_a = refresh(0, ra2[...].reshape(256, 256), hot_a[...].reshape(1024, 256))
    gha[...] = mm(wt[256:1280, :], new_a).astype(BF).reshape(4, 4, 4, 16, 256)
    for step in range(1, 4):
        to = (y + step) % 4
        start(12, gha.at[:, to], rha.at[y], zc, to * 4 + x)
    ga[...] = mm(wt[0:256, :], new_a).astype(BF).reshape(16, 16, 256)
    rga[g] = ga[g]
    along_g(10, ga, rga)
    rha[y] = gha[:, y]

    wait_bytes(rb2.at[pl.ds(0, 15)], recv.at[3])
    wait_bytes(hot_b.at[:, :, pl.ds(0, 3)], recv.at[7])
    rowsb[...] = swap(rb2[...].reshape(256, 256))
    new_b = refresh(1, rowsb[...], hot_b[...].reshape(1024, 256))
    ghb[...] = mm(wt[256:1280, :], new_b).astype(BF).reshape(4, 4, 4, 16, 256)
    for step in range(1, 4):
        to = (x + step) % 4
        start(13, ghb.at[:, :, to], rhb.at[x], zc, y * 4 + to)
    gb[...] = swap(mm(wt[0:256, :], new_b).astype(BF)).reshape(16, 16, 256)
    rgb[zc] = gb[zc]
    along_zc(11, gb, rgb)
    rhb[x] = ghb[:, :, x]

    start(19, nvm, newc_hbm.at[:, half], zc + 1 - 2 * c, g)
    own_copy = pltpu.make_async_copy(nvm, newc_hbm.at[:, half], local.at[2])
    own_copy.start()

    wait_bytes(rga.at[pl.ds(0, 15)], recv.at[10])
    fa[...] = swap(rga[...].reshape(256, 256)).reshape(16, 16, 256)
    rfa[zc] = fa[zc]
    along_zc(14, fa, rfa)

    wait_bytes(rgb.at[pl.ds(0, 15)], recv.at[11])
    fb[...] = swap(rgb[...].reshape(256, 256)).reshape(16, 16, 256)
    rfb[g] = fb[g]
    along_g(15, fb, rfb)

    wait_bytes(rha.at[pl.ds(0, 3)], recv.at[12])
    h2a[...] = (rha[0] + rha[1]) + (rha[2] + rha[3])
    for step in range(1, 4):
        to = (x + step) % 4
        start(16, h2a.at[:, to], rh2a.at[x], zc, y * 4 + to)
    rh2a[x] = h2a[:, x]
    wait_bytes(rhb.at[pl.ds(0, 3)], recv.at[13])
    h2b[...] = (rhb[0] + rhb[1]) + (rhb[2] + rhb[3])
    for step in range(1, 4):
        to = (y + step) % 4
        start(17, h2b.at[:, to], rh2b.at[y], zc, to * 4 + x)
    rh2b[y] = h2b[:, y]

    wait_bytes(rh2a.at[pl.ds(0, 3)], recv.at[16])
    wait_bytes(rh2b.at[pl.ds(0, 3)], recv.at[17])
    back_a = ((rh2a[0] + rh2a[1]) + (rh2a[2] + rh2a[3])).reshape(64, 256)
    back_b = ((rh2b[0] + rh2b[1]) + (rh2b[2] + rh2b[3])).reshape(64, 256)
    back = jnp.concatenate([back_a[:, :128], back_a[:, 128:], back_b[:, :128], back_b[:, 128:]], axis=0)
    ht[...] = swap(back).reshape(16, 16, 128)
    rht[zc] = ht[zc]
    along_zc(18, ht, rht)

    lane = iota((128, 256), 1)
    cold_owner_col = jnp.where(hot_col, -1, owner_col)
    hit_a = owner_at(lane >> 5, lane & 15) == cold_owner_col
    hit_b = owner_at((lane & 15) >> 1, lane >> 4) == cold_owner_col
    wait_bytes(rfa.at[pl.ds(0, 15)], recv.at[14])
    wait_bytes(rfb.at[pl.ds(0, 15)], recv.at[15])
    picked = []
    for cc in range(2):
        picked.append(mm(onehot(hit_a & ((lane >> 4) & 1 == cc)), rfa[...].reshape(256, 256)))
        picked.append(mm(onehot(hit_b & (lane & 1 == cc)), rfb[...].reshape(256, 256)))
    wait_bytes(rht.at[pl.ds(0, 15)], recv.at[18])
    tile_lane = iota((128, 16), 1)
    tiles = []
    for cc in range(2):
        tile = rht[cc]
        for zz in range(1, 8):
            tile = tile + rht[zz * 2 + cc]
        for j in range(4):
            match = (tile_lane >> 2 == j) & ((tile_lane & 3).astype(F32) == slot_col)
            tiles.append(mm(onehot(match), tile))
    near = jnp.concatenate(picked, axis=1) + jnp.concatenate(tiles, axis=1)
    residual = (x_ref[...].astype(F32) - near).astype(BF)
    rot_copy.wait()
    for a in range(4):
        cols = slice(a * 256, a * 256 + 256)
        out_ref[:, cols] = mm(residual, rvm[:, cols]).astype(BF)

    own_copy.wait()
    wait_bytes(newc_hbm.at[:, half], recv.at[19])
    wait_bytes(sbuf.at[pl.ds(0, 7)], send.at[0])
    wait_bytes(sbuf.at[0, 0], send.at[0])
    for stage, ref in ((1, bbuf), (2, a2), (3, b2), (10, ga), (11, gb), (14, fa), (15, fb), (18, ht)):
        wait_bytes(ref.at[pl.ds(0, 15)], send.at[stage])
    wait_bytes(hot_a.at[:, 0, pl.ds(0, 3)], send.at[4])
    wait_bytes(hot_b.at[:, 0, pl.ds(0, 3)], send.at[6])
    wait_bytes(idb.at[0, pl.ds(0, 3)], send.at[8])
    wait_bytes(hot_a.at[:, pl.ds(0, 3)], send.at[5])
    wait_bytes(hot_b.at[:, :, pl.ds(0, 3)], send.at[7])
    wait_bytes(idb.at[pl.ds(0, 3)], send.at[9])
    wait_bytes(gha.at[:, pl.ds(0, 3)], send.at[12])
    wait_bytes(ghb.at[:, :, pl.ds(0, 3)], send.at[13])
    wait_bytes(h2a.at[:, pl.ds(0, 3)], send.at[16])
    wait_bytes(h2b.at[:, pl.ds(0, 3)], send.at[17])
    wait_bytes(nvm, send.at[19])


def per_device(inserts, list_ids, centroids, prior_counts, rotation):
    blocks = [
        pltpu.VMEM(shape, BF)
        for shape in (
            (8, 2, 64, 128), (16, 64, 128), (16, 16, 256), (16, 16, 256), (16, 16, 256), (16, 16, 256),
            (16, 16, 256), (16, 16, 256), (4, 4, 4, 16, 256), (4, 4, 4, 16, 256),
        )
    ]
    work = [
        pltpu.VMEM((4, 4, 16, 128), I32),
        pltpu.VMEM((1024, 1280), BF),
        pltpu.VMEM((1280, 1024), BF),
        pltpu.VMEM((1024, 128), F32),
        pltpu.VMEM((1024, 128), F32),
        pltpu.VMEM((1024, 512), BF),
        pltpu.VMEM((1024, 1024), BF),
        pltpu.VMEM((1024, 512), BF),
        pltpu.VMEM((256, 256), BF),
    ]
    back = [
        pltpu.VMEM(shape, BF)
        for shape in (
            (16, 16, 256), (16, 16, 256), (4, 4, 4, 16, 256), (4, 4, 4, 16, 256), (16, 16, 256), (16, 16, 256),
            (4, 4, 4, 16, 256), (4, 4, 4, 16, 256), (16, 16, 256), (16, 16, 256), (16, 16, 256), (16, 16, 256),
            (4, 4, 16, 256), (4, 4, 16, 256), (4, 4, 16, 256), (4, 4, 16, 256), (16, 16, 128), (16, 16, 128),
            (256, 256),
        )
    ]
    vmem = pl.BlockSpec(memory_space=pltpu.VMEM)
    anywhere = pl.BlockSpec(memory_space=pl.ANY)
    return pl.pallas_call(
        kernel,
        out_shape=(
            jax.ShapeDtypeStruct(centroids.shape, BF),
            jax.ShapeDtypeStruct(inserts.shape, BF),
        ),
        in_specs=[vmem, vmem, vmem, anywhere, anywhere],
        out_specs=(anywhere, vmem),
        scratch_shapes=blocks
        + work
        + back
        + [
            pltpu.SemaphoreType.DMA((STAGES,)),
            pltpu.SemaphoreType.DMA((STAGES,)),
            pltpu.SemaphoreType.DMA((3,)),
        ],
        compiler_params=pltpu.CompilerParams(
            collective_id=0, has_side_effects=True, vmem_limit_bytes=48 * 1024 * 1024
        ),
        cost_estimate=pl.CostEstimate(flops=4_000_000_000, bytes_accessed=8_000_000, transcendentals=0),
    )(list_ids.reshape(1, 128), inserts, prior_counts.reshape(8, 128), centroids, rotation)


def solution(mesh):
    placed = (
        P(("replica", "lists"), None),
        P(("replica", "lists")),
        P("lists", None),
        P("lists"),
        P(),
    )
    return jax.shard_map(
        per_device,
        mesh=mesh,
        in_specs=placed,
        out_specs=(P("lists", None), P(("replica", "lists"), None)),
        check_vma=False,
    )
```

time: 195 us -> 63.4 us (0.33)
  waiting for transfers between devices: 89 us -> 0 us
  Pallas kernels: 0 us -> 56.6 us
  starting transfers between devices: 39.1 us -> 0 us
  local copies, waits for them, and re-layouts: 26.8 us -> 5.9 us
  between operations: 14.3 us -> 0.65 us
  matrix products: 9.61 us -> 0 us
  other arithmetic: 9.14 us -> 0 us
  blocking collectives: 6.31 us -> 0 us
    all_to_all x3 -> x0, waiting for transfers between devices: 60.9 us -> none  [the longest x1 29 us: per_device(): lax.all_to_all(rotated_slots.reshape(owners, slot_size, width), 'lists',...]
    pallas_call x0 -> x1, Pallas kernels: none -> 56.6 us  [per_device(): pl.pallas_call(kernel, out_shape=(jax.ShapeDtypeStruct(centroids.shape, B...]
    all_to_all x3 -> x0, starting transfers between devices: 39.1 us -> none  [the longest x1 16.3 us: per_device(): lax.all_to_all(send_ids, 'lists', split_axis=0, concat_axis=0, tiled=True)]
    psum x1 -> x0, waiting for transfers between devices: 28.1 us -> none  [per_device(): total_sums, total_counts = lax.psum((sums, counts), 'replica')]
    gather x5 -> x0, local copies, waits for them, and re-layouts: 12.8 us -> none  [the longest x1 4.59 us: per_device(): picked = new_centroids[safe_ids].astype(jnp.float32)]
    dot_general x5 -> x0, matrix products: 9.61 us -> none  [the longest x4 5.77 us: accumulate_slots(): jnp.dot(matches.astype(jnp.bfloat16), block_rows, preferred_element_type=...]
    slice x6 -> x0, local copies, waits for them, and re-layouts: 6.55 us -> none  [the longest x5 6.39 us: accumulate_slots(): block_rows = rows_flat[block * block_size:(block + 1) * block_size]]
    psum x1 -> x0, blocking collectives: 6.31 us -> none  [per_device(): total_sums, total_counts = lax.psum((sums, counts), 'replica')]
  transfers between devices with their start and end apart: 4 -> 0, of which waited for: 4 -> 0; matrix products, arithmetic and copies ran while one was open for 5% -> 0% of each run, Pallas kernels for 0% -> 0%
where the time goes in v1:
time: 63.4 us; the launch traced here: 63.2 us
  Pallas kernels  56.6 us (89%)
  local copies, waits for them, and re-layouts  5.9 us (9%)
  between operations  0.65 us (1%)
    pallas_call x1, Pallas kernels, per_device(): pl.pallas_call(kernel, out_shape=(jax.ShapeDtypeStruct(centroids.shape, B...  56.6 us
    unnamed x10, local copies, waits for them, and re-layouts  5.9 us

profile of v1, /device:TPU:1, one launch (start us, length us, event | category | flops | bytes accessed | tf_op | source)
XLA Modules:
  0.0 63.2 jit_solution(16038894367483723955)
XLA Ops:
  0.6 0.0 copy-start
  0.6 1.6 %copy-done = bf16[1024,1024]{1,0:T(8,128)(2,1)S(1)} copy-done((bf16[1024,1024]{1,0:T(8,128)(2,1)S(1)}, bf16[1024,1024]{1,0:T(8,128)(2,1)}, u32[]{:S(2)}) %copy-start) | copy-done | bytes 2097176
  2.2 0.0 copy-start.1
  2.2 0.9 %copy-done.1 = bf16[128,1024]{1,0:T(8,128)(2,1)S(1)} copy-done((bf16[128,1024]{1,0:T(8,128)(2,1)S(1)}, bf16[128,1024]{1,0:T(8,128)(2,1)}, u32[]{:S(2)}) %copy-start.1) | copy-done | bytes 262168
  3.2 0.0 copy-start.2
  3.2 0.7 %copy-done.2 = s32[1024]{0:T(1024)S(1)} copy-done((s32[1024]{0:T(1024)S(1)}, s32[1024]{0:T(1024)}, u32[]{:S(2)}) %copy-start.2) | copy-done | bytes 4120
  3.9 0.0 copy-start.3
  3.9 0.7 %copy-done.3 = s32[128]{0:T(128)S(1)} copy-done((s32[128]{0:T(128)S(1)}, s32[128]{0:T(128)}, u32[]{:S(2)}) %copy-start.3) | copy-done | bytes 536
  4.5 56.6 %shard_map.68 = (bf16[1024,1024]{1,0:T(8,128)(2,1)S(1)}, bf16[128,1024]{1,0:T(8,128)(2,1)S(1)}) custom-call(s32[1,128]{1,0:T(1,128)S(1)} %bitcast.3, bf16[128,1024]{1,0:T(8,128)(2,1)S(1)} %copy-done.1, s32[8,128]{1,0:T(8,128)S(1)} %bitcast.2, bf16[1024,1024]{1,0:T(8,128)(2,1)S(1)} %copy-done, bf16[1024,1024]{1,0:T(8,128)(2,1)} %rot_hbm.1), custom_call_target="tpu_custom_call" | custom-call | flops 4000000000 | bytes 8000000 | tf_op jit(solution)/shard_map/pallas_call | solution.py:357
  61.2 1.3 %copy.9 = bf16[1024,1024]{1,0:T(8,128)(2,1)} copy(bf16[1024,1024]{1,0:T(8,128)(2,1)S(1)} %get-tuple-element.4) | data formatting | bytes 4194304
  62.5 0.7 %copy.10 = bf16[128,1024]{1,0:T(8,128)(2,1)} copy(bf16[128,1024]{1,0:T(8,128)(2,1)S(1)} %get-tuple-element.5) | data formatting | bytes 524288
Async XLA Ops:
  0.6 1.6 %copy-start = (bf16[1024,1024]{1,0:T(8,128)(2,1)S(1)}, bf16[1024,1024]{1,0:T(8,128)(2,1)}, u32[]{:S(2)}) copy-start(bf16[1024,1024]{1,0:T(8,128)(2,1)} %cent_hbm.1) | copy-start | bytes 6291460
  2.2 0.9 %copy-start.1 = (bf16[128,1024]{1,0:T(8,128)(2,1)S(1)}, bf16[128,1024]{1,0:T(8,128)(2,1)}, u32[]{:S(2)}) copy-start(bf16[128,1024]{1,0:T(8,128)(2,1)} %x_ref.1) | copy-start | bytes 786436
  3.2 0.7 %copy-start.2 = (s32[1024]{0:T(1024)S(1)}, s32[1024]{0:T(1024)}, u32[]{:S(2)}) copy-start(s32[1024]{0:T(1024)} %param.8) | copy-start | bytes 12292
  3.9 0.7 %copy-start.3 = (s32[128]{0:T(128)S(1)}, s32[128]{0:T(128)}, u32[]{:S(2)}) copy-start(s32[128]{0:T(128)} %param.6) | copy-start | bytes 1540

commit v2 on v1

v2 whole, which is shorter than its diff:
```python
import jax
import jax.numpy as jnp
from jax import lax
from jax.experimental import pallas as pl
from jax.experimental.pallas import tpu as pltpu
from jax.sharding import PartitionSpec as P

MESH = pl.DeviceIdType.MESH
BF = jnp.bfloat16
F32 = jnp.float32
I32 = jnp.int32
STAGES = 21


def mm(a, b):
    return jnp.dot(a, b, preferred_element_type=F32)


def iota(shape, dim):
    return lax.broadcasted_iota(I32, shape, dim)


def onehot(mask):
    return jnp.where(mask, 1.0, 0.0).astype(BF)


def owner_at(zz, gg):
    return (zz << 4) + ((gg & 3) << 2) + (gg >> 2)


def wait_bytes(ref, sem):
    pltpu.make_async_copy(ref, ref, sem).wait()


def kernel(
    ids_hbm, x_hbm, prior_hbm, cent_hbm, rot_hbm, newc_hbm, out_ref,
    ids_ref, x_ref, prior_ref, hbuf, hr, abuf, ra, bbuf, rb1, a2, ra2, b2, rb2, hot_a, hot_b, idb,
    w, wt, cnt, rinv, cvm, rvm, nvm, acc,
    ga, gb, gha, ghb, rga, rgb, rha, rhb, fa, fb, rfa, rfb,
    h2a, h2b, rh2a, rh2b, ht, rht, perm, send, recv, local,
):
    c = lax.axis_index("replica")
    li = lax.axis_index("lists")
    z = li // 16
    x = (li // 4) % 4
    y = li % 4
    zc = z * 2 + c
    g = y * 4 + x


    moved_by = {
        0: [ra.at[pl.ds(0, 15)]], 20: [hr.at[pl.ds(0, 15)]], 1: [bbuf.at[pl.ds(0, 15)]], 2: [a2.at[pl.ds(0, 15)]], 3: [b2.at[pl.ds(0, 15)]],
        4: [hot_a.at[:, 0, pl.ds(0, 3)]], 5: [hot_a.at[:, pl.ds(0, 3)]], 6: [hot_b.at[:, 0, pl.ds(0, 3)]],
        7: [hot_b.at[:, :, pl.ds(0, 3)]], 8: [idb.at[0, pl.ds(0, 3)]], 9: [idb.at[pl.ds(0, 3)]],
        10: [ga.at[pl.ds(0, 15)]], 11: [gb.at[pl.ds(0, 15)]], 12: [gha.at[:, pl.ds(0, 3)]], 13: [ghb.at[:, :, pl.ds(0, 3)]],
        14: [fa.at[pl.ds(0, 15)]], 15: [fb.at[pl.ds(0, 15)]], 16: [h2a.at[:, pl.ds(0, 3)]], 17: [h2b.at[:, pl.ds(0, 3)]],
        18: [ht.at[pl.ds(0, 15)]], 19: [nvm],
    }
    started, arrived = [], []

    def arrive(stage):
        arrived.append(stage)
        for ref in moved_by[stage]:
            wait_bytes(ref, recv.at[stage])

    def finish():
        for stage in dict.fromkeys(started):
            if stage not in arrived:
                arrive(stage)
            for ref in moved_by[stage]:
                wait_bytes(ref, send.at[stage])

    def dev(zc_to, g_to):
        return (zc_to % 2, (zc_to // 2) * 16 + (g_to % 4) * 4 + g_to // 4)

    def start(stage, src, dst, zc_to, g_to):
        started.append(stage)
        pltpu.make_async_remote_copy(
            src_ref=src, dst_ref=dst, send_sem=send.at[stage], recv_sem=recv.at[stage],
            device_id=dev(zc_to, g_to), device_id_type=MESH,
        ).start()

    def along_zc(stage, src, dst):
        @pl.loop(1, 16)
        def _(step):
            to = (zc + step) % 16
            start(stage, src.at[to], dst.at[zc], to, g)

    def along_g(stage, src, dst):
        @pl.loop(1, 16)
        def _(step):
            to = (g + step) % 16
            start(stage, src.at[to], dst.at[g], zc, to)

    barrier = pltpu.get_barrier_semaphore()

    @pl.loop(1, 16)
    def _(step):
        pl.semaphore_signal(barrier, 1, device_id=dev((zc + step) % 16, g), device_id_type=MESH)
        pl.semaphore_signal(barrier, 1, device_id=dev(zc, (g + step) % 16), device_id_type=MESH)

    half = pl.ds(pl.multiple_of(c * 512, 512), 512)
    copies = [
        pltpu.make_async_copy(src, dst, local.at[n])
        for n, (src, dst) in enumerate(
            ((ids_hbm, ids_ref), (x_hbm, x_ref), (prior_hbm, prior_ref), (cent_hbm.at[:, half], cvm), (rot_hbm, rvm))
        )
    ]
    for copy in copies:
        copy.start()
    copies[0].wait()

    ids = ids_ref[...]
    owner_row = ids >> 10
    eye = iota((128, 128), 0) == iota((128, 128), 1)
    owner_col = jnp.sum(jnp.where(eye, owner_row, 0), axis=1, keepdims=True)
    same = jnp.where(owner_col == owner_row, 1.0, 0.0)
    earlier = jnp.where(iota((128, 128), 0) < iota((128, 128), 1), same, 0.0)
    later = jnp.where(iota((128, 128), 1) < iota((128, 128), 0), same, 0.0)
    rank_row = jnp.sum(earlier, axis=0, keepdims=True)
    rank_col = jnp.sum(later, axis=1, keepdims=True)
    cold_owner_row = jnp.where(rank_row > 0.5, -1, owner_row)
    cold_owner_col = jnp.where(rank_col > 0.5, -1, owner_col)

    tile_row = iota((16, 128), 0)
    info = jnp.where(tile_row == 12, owner_row, 0)
    info = jnp.where(tile_row == 13, (ids & 1023) >> 5, info)
    info = jnp.where(tile_row == 14, ids & 31, info).astype(F32)
    info = jnp.where(tile_row == 15, rank_row, info)
    copies[1].wait()
    for cc in range(2):
        tile = info
        for j in range(4):
            match = (tile_row >= j * 3) & (tile_row < j * 3 + 3) & ((tile_row - (j * 3 - 1)).astype(F32) == rank_row)
            low = cc * 512 + j * 128
            tile = tile + mm(onehot(match), x_ref[:, low : low + 128])
        hbuf[cc] = tile.astype(BF)
    p0, p1 = iota((256, 256), 0), iota((256, 256), 1)
    perm[...] = onehot((p0 >> 4 == p1 & 15) & (p0 & 15 == p1 >> 4))

    def swap(rows):
        return mm(perm[...], rows).astype(BF)

    hr[zc] = hbuf[c]
    pl.semaphore_wait(barrier, 30)

    @pl.loop(1, 16)
    def _(step):
        to = (zc + step) % 16
        start(20, hbuf.at[to % 2], hr.at[zc], to, g)

    r128 = iota((128, 128), 0)
    pick = onehot(owner_at(r128 >> 4, r128 & 15) == cold_owner_row)
    for cc in range(2):
        block = mm(pick, x_ref[:, cc * 512 : cc * 512 + 256]).astype(BF)
        abuf[:, cc] = block.reshape(8, 16, 256)
    ra[zc] = abuf[z, c]

    @pl.loop(1, 16)
    def _(step):
        to = (zc + step) % 16
        start(0, abuf.at[to // 2, to % 2], ra.at[zc], to, g)

    r256 = iota((256, 128), 0)
    hit = owner_at((r256 & 15) >> 1, r256 >> 4) == cold_owner_row
    part_b = mm(onehot(hit & ((r256 & 1) == 0)), x_ref[:, 256:512])
    part_b = part_b + mm(onehot(hit & ((r256 & 1) == 1)), x_ref[:, 768:1024])
    bbuf[...] = part_b.astype(BF).reshape(16, 16, 256)
    rb1[g] = bbuf[g]
    along_g(1, bbuf, rb1)

    copies[2].wait()
    ones = jnp.ones((128, 128), BF)
    for a in range(8):
        diag = jnp.where(eye, prior_ref[a : a + 1, :].astype(F32), 0.0).astype(BF)
        rinv[a * 128 : a * 128 + 128, :] = mm(diag, ones)

    arrive(20)
    hot_rows = mm(perm[...], hr[...].reshape(256, 128))
    hot = hot_rows.astype(BF)
    for j, (ref, low) in enumerate(((hot_a, 0), (hot_a, 128), (hot_b, 0), (hot_b, 128))):
        ref[:, y, x, :, low : low + 128] = hot[j * 48 : j * 48 + 48].reshape(3, 16, 128)
    got = hot_rows[192:256].astype(I32)
    idb[y, x] = (got[48:64] << 17) + (got[0:16] << 10) + (got[16:32] << 5) + got[32:48]
    for step in range(1, 4):
        to = y * 4 + (x + step) % 4
        start(8, idb.at[y, x], idb.at[y, x], zc, to)
        start(4, hot_a.at[:, y, x], hot_a.at[:, y, x], zc, to)
        start(6, hot_b.at[:, y, x], hot_b.at[:, y, x], zc, ((y + step) % 4) * 4 + x)

    arrive(0)
    a2[...] = swap(ra[...].reshape(256, 256)).reshape(16, 16, 256)
    ra2[g] = a2[g]
    along_g(2, a2, ra2)

    arrive(1)
    b2[...] = swap(rb1[...].reshape(256, 256)).reshape(16, 16, 256)
    rb2[zc] = b2[zc]
    along_zc(3, b2, rb2)

    arrive(8)
    arrive(4)
    arrive(6)
    for step in range(1, 4):
        to = ((y + step) % 4) * 4 + x
        start(9, idb.at[y], idb.at[y], zc, to)
        start(5, hot_a.at[:, y], hot_a.at[:, y], zc, to)
        start(7, hot_b.at[:, :, x], hot_b.at[:, :, x], zc, y * 4 + (x + step) % 4)

    arrive(9)
    code = idb[...].reshape(256, 128)
    mine = ((code >> 10) & 127) == li
    slot = code >> 17
    number = (code & 1023) + 1
    ones8 = jnp.ones((8, 256), BF)
    ones256 = jnp.ones((256, 128), BF)
    for block, s in enumerate((0, 1, 2, 3)):
        here = mine & (slot == s)
        top = jnp.where(here, number & 2016, 0).astype(F32).astype(BF)
        low = jnp.where(here, number & 31, 0).astype(F32).astype(BF)
        both = jnp.concatenate([top, low], axis=1)
        lanes = lax.dot_general(ones8, both, (((1,), (1,)), ((), ())), preferred_element_type=F32)
        lanes = lanes.astype(I32)[0:1, :] - 1
        rows = mm(both, ones256).astype(I32) - 1
        for a in range(8):
            w[a * 128 : a * 128 + 128, block * 256 : block * 256 + 256] = onehot(
                iota((128, 256), 0) + a * 128 == lanes
            )
            wt[block * 256 : block * 256 + 256, a * 128 : a * 128 + 128] = onehot(
                iota((256, 128), 1) + a * 128 == rows
            )
    for a in range(4):
        lists = slice(a * 256, a * 256 + 256)
        total = mm(w[lists, :], jnp.ones((1024, 128), BF))
        cnt[lists, :] = total
        rinv[lists, :] = 1.0 / (rinv[lists, :] + total)

    def begin(part, cold):
        for a in range(4):
            lists = slice(a * 256, a * 256 + 256)
            old = cvm[lists, part * 256 : part * 256 + 256].astype(F32)
            count = jnp.concatenate([cnt[lists, :]] * 2, axis=1)
            acc[part, lists, :] = mm(w[lists, 0:256], cold) - count * old

    def refresh(part, hot_rows):
        cols = slice(part * 256, part * 256 + 256)
        for a in range(4):
            lists = slice(a * 256, a * 256 + 256)
            change = acc[part, lists, :] + mm(w[lists, 256:1024], hot_rows)
            scale = jnp.concatenate([rinv[lists, :]] * 2, axis=1)
            nvm[lists, cols] = (cvm[lists, cols].astype(F32) + change * scale).astype(BF)
        return nvm[:, cols]

    copies[3].wait()
    arrive(2)
    begin(0, ra2[...].reshape(256, 256))
    arrive(3)
    begin(1, swap(rb2[...].reshape(256, 256)))

    arrive(5)
    new_a = refresh(0, hot_a[...].reshape(768, 256))
    gha[...] = mm(wt[256:1024, :], new_a).astype(BF).reshape(3, 4, 4, 16, 256)
    for step in range(1, 4):
        to = (y + step) % 4
        start(12, gha.at[:, to], rha.at[y], zc, to * 4 + x)
    arrive(7)
    new_b = refresh(1, hot_b[...].reshape(768, 256))
    ghb[...] = mm(wt[256:1024, :], new_b).astype(BF).reshape(3, 4, 4, 16, 256)
    for step in range(1, 4):
        to = (x + step) % 4
        start(13, ghb.at[:, :, to], rhb.at[x], zc, y * 4 + to)
    ga[...] = mm(wt[0:256, :], new_a).astype(BF).reshape(16, 16, 256)
    rga[g] = ga[g]
    along_g(10, ga, rga)
    gb[...] = swap(mm(wt[0:256, :], new_b).astype(BF)).reshape(16, 16, 256)
    rgb[zc] = gb[zc]
    along_zc(11, gb, rgb)
    rha[y] = gha[:, y]
    rhb[x] = ghb[:, :, x]

    start(19, nvm, newc_hbm.at[:, half], zc + 1 - 2 * c, g)
    own_copy = pltpu.make_async_copy(nvm, newc_hbm.at[:, half], local.at[5])
    own_copy.start()

    arrive(12)
    h2a[...] = (rha[0] + rha[1]) + (rha[2] + rha[3])
    for step in range(1, 4):
        to = (x + step) % 4
        start(16, h2a.at[:, to], rh2a.at[x], zc, y * 4 + to)
    rh2a[x] = h2a[:, x]
    arrive(13)
    h2b[...] = (rhb[0] + rhb[1]) + (rhb[2] + rhb[3])
    for step in range(1, 4):
        to = (y + step) % 4
        start(17, h2b.at[:, to], rh2b.at[y], zc, to * 4 + x)
    rh2b[y] = h2b[:, y]

    arrive(10)
    fa[...] = swap(rga[...].reshape(256, 256)).reshape(16, 16, 256)
    rfa[zc] = fa[zc]
    along_zc(14, fa, rfa)
    arrive(11)
    fb[...] = swap(rgb[...].reshape(256, 256)).reshape(16, 16, 256)
    rfb[g] = fb[g]
    along_g(15, fb, rfb)

    arrive(16)
    arrive(17)
    back_a = ((rh2a[0] + rh2a[1]) + (rh2a[2] + rh2a[3])).reshape(48, 256)
    back_b = ((rh2b[0] + rh2b[1]) + (rh2b[2] + rh2b[3])).reshape(48, 256)
    back = jnp.concatenate(
        [back_a[:, :128], back_a[:, 128:], back_b[:, :128], back_b[:, 128:], jnp.zeros((64, 128), BF)], axis=0
    )
    ht[...] = swap(back).reshape(16, 16, 128)
    rht[zc] = ht[zc]
    along_zc(18, ht, rht)

    lane = iota((128, 256), 1)
    hit_a = owner_at(lane >> 5, lane & 15) == cold_owner_col
    hit_b = owner_at((lane & 15) >> 1, lane >> 4) == cold_owner_col
    arrive(14)
    arrive(15)
    picked = []
    for cc in range(2):
        picked.append(mm(onehot(hit_a & ((lane >> 4) & 1 == cc)), rfa[...].reshape(256, 256)))
        picked.append(mm(onehot(hit_b & (lane & 1 == cc)), rfb[...].reshape(256, 256)))
    arrive(18)
    tile_lane = iota((128, 16), 1)
    tiles = []
    for cc in range(2):
        tile = rht[cc]
        for zz in range(1, 8):
            tile = tile + rht[zz * 2 + cc]
        for j in range(4):
            match = (tile_lane >= j * 3) & (tile_lane < j * 3 + 3) & ((tile_lane - (j * 3 - 1)).astype(F32) == rank_col)
            tiles.append(mm(onehot(match), tile))
    near = jnp.concatenate(picked, axis=1) + jnp.concatenate(tiles, axis=1)
    residual = (x_ref[...].astype(F32) - near).astype(BF)
    copies[4].wait()
    for a in range(4):
        cols = slice(a * 256, a * 256 + 256)
        out_ref[:, cols] = mm(residual, rvm[:, cols]).astype(BF)

    own_copy.wait()
    finish()


def per_device(inserts, list_ids, centroids, prior_counts, rotation):
    square, tall, plane = (16, 16, 256), (3, 4, 4, 16, 256), (4, 3, 16, 256)
    shapes = [
        (2, 16, 128), (16, 16, 128), (8, 2, 16, 256), square, square, square, square, square, square, square, tall, tall,
        None, (1024, 1024), (1024, 1024), None, None, (1024, 512), (1024, 1024), (1024, 512), None,
        square, square, tall, tall, square, square, (4, 3, 4, 16, 256), (4, 3, 4, 16, 256), square, square, square, square,
        (3, 4, 16, 256), (3, 4, 16, 256), plane, plane, (16, 16, 128), (16, 16, 128), (256, 256),
    ]
    others = [
        pltpu.VMEM((4, 4, 16, 128), I32),
        pltpu.VMEM((1024, 128), F32),
        pltpu.VMEM((1024, 128), F32),
        pltpu.VMEM((2, 1024, 256), F32),
    ]
    scratch = [pltpu.VMEM(shape, BF) if shape else others.pop(0) for shape in shapes]
    given = [pltpu.VMEM((1, 128), I32), pltpu.VMEM(inserts.shape, BF), pltpu.VMEM((8, 128), I32)]
    vmem = pl.BlockSpec(memory_space=pltpu.VMEM)
    anywhere = pl.BlockSpec(memory_space=pl.ANY)
    return pl.pallas_call(
        kernel,
        out_shape=(
            jax.ShapeDtypeStruct(centroids.shape, BF),
            jax.ShapeDtypeStruct(inserts.shape, BF),
        ),
        in_specs=[pl.BlockSpec(memory_space=pltpu.HBM)] * 5,
        out_specs=(anywhere, vmem),
        scratch_shapes=given
        + scratch
        + [
            pltpu.SemaphoreType.DMA((STAGES,)),
            pltpu.SemaphoreType.DMA((STAGES,)),
            pltpu.SemaphoreType.DMA((6,)),
        ],
        compiler_params=pltpu.CompilerParams(
            collective_id=0, has_side_effects=True, vmem_limit_bytes=48 * 1024 * 1024
        ),
        cost_estimate=pl.CostEstimate(flops=4_000_000_000, bytes_accessed=8_000_000, transcendentals=0),
    )(list_ids.reshape(1, 128), inserts, prior_counts.reshape(8, 128), centroids, rotation)


def solution(mesh):
    placed = (
        P(("replica", "lists"), None),
        P(("replica", "lists")),
        P("lists", None),
        P("lists"),
        P(),
    )
    return jax.shard_map(
        per_device,
        mesh=mesh,
        in_specs=placed,
        out_specs=(P("lists", None), P(("replica", "lists"), None)),
        check_vma=False,
    )
```

time: 63.4 us -> 56.7 us (0.89)
  Pallas kernels: 56.6 us -> 49.9 us
    pallas_call x1, Pallas kernels: 56.6 us -> 49.9 us  [per_device(): pl.pallas_call(kernel, out_shape=(jax.ShapeDtypeStruct(centroids.shape, B...]
where the time goes in v2:
time: 56.7 us; the launch traced here: 56.5 us
  Pallas kernels  49.9 us (88%)
  local copies, waits for them, and re-layouts  5.9 us (10%)
  between operations  0.65 us (1%)
    pallas_call x1, Pallas kernels, per_device(): pl.pallas_call(kernel, out_shape=(jax.ShapeDtypeStruct(centroids.shape, B...  49.9 us
    unnamed x10, local copies, waits for them, and re-layouts  5.9 us

profile of v2, /device:TPU:1, one launch (start us, length us, event | category | flops | bytes accessed | tf_op | source)
XLA Modules:
  0.0 56.5 jit_solution(11655226915481031687)
XLA Ops:
  0.6 0.0 copy-start
  0.6 1.6 %copy-done = bf16[1024,1024]{1,0:T(8,128)(2,1)S(1)} copy-done((bf16[1024,1024]{1,0:T(8,128)(2,1)S(1)}, bf16[1024,1024]{1,0:T(8,128)(2,1)}, u32[]{:S(2)}) %copy-start) | copy-done | bytes 2097176
  2.2 0.0 copy-start.1
  2.2 0.9 %copy-done.1 = bf16[128,1024]{1,0:T(8,128)(2,1)S(1)} copy-done((bf16[128,1024]{1,0:T(8,128)(2,1)S(1)}, bf16[128,1024]{1,0:T(8,128)(2,1)}, u32[]{:S(2)}) %copy-start.1) | copy-done | bytes 262168
  3.2 0.0 copy-start.2
  3.2 0.7 %copy-done.2 = s32[1024]{0:T(1024)S(1)} copy-done((s32[1024]{0:T(1024)S(1)}, s32[1024]{0:T(1024)}, u32[]{:S(2)}) %copy-start.2) | copy-done | bytes 4120
  3.9 0.0 copy-start.3
  3.9 0.7 %copy-done.3 = s32[128]{0:T(128)S(1)} copy-done((s32[128]{0:T(128)S(1)}, s32[128]{0:T(128)}, u32[]{:S(2)}) %copy-start.3) | copy-done | bytes 536
  4.5 49.9 %shard_map.68 = (bf16[1024,1024]{1,0:T(8,128)(2,1)S(1)}, bf16[128,1024]{1,0:T(8,128)(2,1)S(1)}) custom-call(s32[1,128]{1,0:T(1,128)S(1)} %bitcast.3, bf16[128,1024]{1,0:T(8,128)(2,1)S(1)} %copy-done.1, s32[8,128]{1,0:T(8,128)S(1)} %bitcast.2, bf16[1024,1024]{1,0:T(8,128)(2,1)S(1)} %copy-done, bf16[1024,1024]{1,0:T(8,128)(2,1)} %rot_hbm.1), custom_call_target="tpu_custom_call" | custom-call | flops 4000000000 | bytes 8000000 | tf_op jit(solution)/shard_map/pallas_call | solution.py:366
  54.4 1.3 %copy.9 = bf16[1024,1024]{1,0:T(8,128)(2,1)} copy(bf16[1024,1024]{1,0:T(8,128)(2,1)S(1)} %get-tuple-element.4) | data formatting | bytes 4194304
  55.8 0.7 %copy.10 = bf16[128,1024]{1,0:T(8,128)(2,1)} copy(bf16[128,1024]{1,0:T(8,128)(2,1)S(1)} %get-tuple-element.5) | data formatting | bytes 524288
Async XLA Ops:
  0.6 1.6 %copy-start = (bf16[1024,1024]{1,0:T(8,128)(2,1)S(1)}, bf16[1024,1024]{1,0:T(8,128)(2,1)}, u32[]{:S(2)}) copy-start(bf16[1024,1024]{1,0:T(8,128)(2,1)} %cent_hbm.1) | copy-start | bytes 6291460
  2.2 0.9 %copy-start.1 = (bf16[128,1024]{1,0:T(8,128)(2,1)S(1)}, bf16[128,1024]{1,0:T(8,128)(2,1)}, u32[]{:S(2)}) copy-start(bf16[128,1024]{1,0:T(8,128)(2,1)} %x_hbm.1) | copy-start | bytes 786436
  3.2 0.7 %copy-start.2 = (s32[1024]{0:T(1024)S(1)}, s32[1024]{0:T(1024)}, u32[]{:S(2)}) copy-start(s32[1024]{0:T(1024)} %param.8) | copy-start | bytes 12292
  3.9 0.7 %copy-start.3 = (s32[128]{0:T(128)S(1)}, s32[128]{0:T(128)}, u32[]{:S(2)}) copy-start(s32[128]{0:T(128)} %param.6) | copy-start | bytes 1540

commit v3 on v2

--- a/solution.py
+++ b/solution.py
@@ -35,7 +35,7 @@
 def kernel(
     ids_hbm, x_hbm, prior_hbm, cent_hbm, rot_hbm, newc_hbm, out_ref,
     ids_ref, x_ref, prior_ref, hbuf, hr, abuf, ra, bbuf, rb1, a2, ra2, b2, rb2, hot_a, hot_b, idb,
-    w, wt, cnt, rinv, cvm, rvm, nvm, acc,
+    w, wt, mates, crow, prior_of, rowsb, nrow, irow, cvm, rvm, nvm, acc,
     ga, gb, gha, ghb, rga, rgb, rha, rhb, fa, fb, rfa, rfb,
     h2a, h2b, rh2a, rh2b, ht, rht, perm, send, recv, local,
 ):
@@ -51,7 +51,7 @@
     moved_by = {
         0: [ra.at[pl.ds(0, 15)]], 20: [hr.at[pl.ds(0, 15)]], 1: [bbuf.at[pl.ds(0, 15)]], 2: [a2.at[pl.ds(0, 15)]], 3: [b2.at[pl.ds(0, 15)]],
         4: [hot_a.at[:, 0, pl.ds(0, 3)]], 5: [hot_a.at[:, pl.ds(0, 3)]], 6: [hot_b.at[:, 0, pl.ds(0, 3)]],
-        7: [hot_b.at[:, :, pl.ds(0, 3)]], 8: [idb.at[0, pl.ds(0, 3)]], 9: [idb.at[pl.ds(0, 3)]],
+        7: [hot_b.at[:, :, pl.ds(0, 3)]], 8: [idb.at[pl.ds(0, 15)]],
         10: [ga.at[pl.ds(0, 15)]], 11: [gb.at[pl.ds(0, 15)]], 12: [gha.at[:, pl.ds(0, 3)]], 13: [ghb.at[:, :, pl.ds(0, 3)]],
         14: [fa.at[pl.ds(0, 15)]], 15: [fb.at[pl.ds(0, 15)]], 16: [h2a.at[:, pl.ds(0, 3)]], 17: [h2b.at[:, pl.ds(0, 3)]],
         18: [ht.at[pl.ds(0, 15)]], 19: [nvm],
@@ -173,7 +173,7 @@
     ones = jnp.ones((128, 128), BF)
     for a in range(8):
         diag = jnp.where(eye, prior_ref[a : a + 1, :].astype(F32), 0.0).astype(BF)
-        rinv[a * 128 : a * 128 + 128, :] = mm(diag, ones)
+        prior_of[a * 128 : a * 128 + 128, :] = mm(diag, ones).astype(BF)
 
     arrive(20)
     hot_rows = mm(perm[...], hr[...].reshape(256, 128))
@@ -181,10 +181,14 @@
     for j, (ref, low) in enumerate(((hot_a, 0), (hot_a, 128), (hot_b, 0), (hot_b, 128))):
         ref[:, y, x, :, low : low + 128] = hot[j * 48 : j * 48 + 48].reshape(3, 16, 128)
     got = hot_rows[192:256].astype(I32)
-    idb[y, x] = (got[48:64] << 17) + (got[0:16] << 10) + (got[16:32] << 5) + got[32:48]
+    idb[g] = (got[48:64] << 17) + (got[0:16] << 10) + (got[16:32] << 5) + got[32:48]
+
+    @pl.loop(1, 16)
+    def _(step):
+        start(8, idb.at[g], idb.at[g], zc, (g + step) % 16)
+
     for step in range(1, 4):
         to = y * 4 + (x + step) % 4
-        start(8, idb.at[y, x], idb.at[y, x], zc, to)
         start(4, hot_a.at[:, y, x], hot_a.at[:, y, x], zc, to)
         start(6, hot_b.at[:, y, x], hot_b.at[:, y, x], zc, ((y + step) % 4) * 4 + x)
 
@@ -198,89 +202,88 @@
     rb2[zc] = b2[zc]
     along_zc(3, b2, rb2)
 
-    arrive(8)
     arrive(4)
     arrive(6)
     for step in range(1, 4):
         to = ((y + step) % 4) * 4 + x
-        start(9, idb.at[y], idb.at[y], zc, to)
         start(5, hot_a.at[:, y], hot_a.at[:, y], zc, to)
         start(7, hot_b.at[:, :, x], hot_b.at[:, :, x], zc, y * 4 + (x + step) % 4)
 
-    arrive(9)
+    arrive(8)
     code = idb[...].reshape(256, 128)
     mine = ((code >> 10) & 127) == li
-    slot = code >> 17
+    rank = code >> 17
     number = (code & 1023) + 1
     ones8 = jnp.ones((8, 256), BF)
     ones256 = jnp.ones((256, 128), BF)
-    for block, s in enumerate((0, 1, 2, 3)):
-        here = mine & (slot == s)
+    lanes, rows = [], []
+    for s in range(4):
+        here = mine & (rank == s)
         top = jnp.where(here, number & 2016, 0).astype(F32).astype(BF)
         low = jnp.where(here, number & 31, 0).astype(F32).astype(BF)
         both = jnp.concatenate([top, low], axis=1)
-        lanes = lax.dot_general(ones8, both, (((1,), (1,)), ((), ())), preferred_element_type=F32)
-        lanes = lanes.astype(I32)[0:1, :] - 1
-        rows = mm(both, ones256).astype(I32) - 1
+        lane = lax.dot_general(ones8, both, (((1,), (1,)), ((), ())), preferred_element_type=F32)
+        lane = lane.astype(I32)[0:1, :]
+        lanes.append(jnp.where(lane == 0, -2, lane - 1))
+        rows.append(mm(both, ones256).astype(I32) - 1)
+    copies[3].wait()
+    for s in range(4):
+        block = slice(s * 256, s * 256 + 256)
         for a in range(8):
-            w[a * 128 : a * 128 + 128, block * 256 : block * 256 + 256] = onehot(
-                iota((128, 256), 0) + a * 128 == lanes
-            )
-            wt[block * 256 : block * 256 + 256, a * 128 : a * 128 + 128] = onehot(
-                iota((256, 128), 1) + a * 128 == rows
-            )
-    for a in range(4):
-        lists = slice(a * 256, a * 256 + 256)
-        total = mm(w[lists, :], jnp.ones((1024, 128), BF))
-        cnt[lists, :] = total
-        rinv[lists, :] = 1.0 / (rinv[lists, :] + total)
+            wt[block, a * 128 : a * 128 + 128] = onehot(iota((256, 128), 1) + a * 128 == rows[s])
+        for t in range(4):
+            for h in range(2):
+                low = t * 256 + h * 128
+                mates[block, low : low + 128] = onehot(rows[s] == lanes[t][:, h * 128 : h * 128 + 128])
+        crow[block, :] = mm(wt[block, :], cvm[...]).astype(BF)
+        total = mm(mates[block, :], jnp.ones((1024, 128), BF))
+        nrow[block, :] = total
+        irow[block, :] = 1.0 / jnp.maximum(mm(wt[block, :], prior_of[...]) + total, 1.0)
+
+    def twice(rows128):
+        return jnp.concatenate([rows128] * 2, axis=1)
 
     def begin(part, cold):
-        for a in range(4):
-            lists = slice(a * 256, a * 256 + 256)
-            old = cvm[lists, part * 256 : part * 256 + 256].astype(F32)
-            count = jnp.concatenate([cnt[lists, :]] * 2, axis=1)
-            acc[part, lists, :] = mm(w[lists, 0:256], cold) - count * old
-
-    def refresh(part, hot_rows):
         cols = slice(part * 256, part * 256 + 256)
         for a in range(4):
-            lists = slice(a * 256, a * 256 + 256)
-            change = acc[part, lists, :] + mm(w[lists, 256:1024], hot_rows)
-            scale = jnp.concatenate([rinv[lists, :]] * 2, axis=1)
-            nvm[lists, cols] = (cvm[lists, cols].astype(F32) + change * scale).astype(BF)
-        return nvm[:, cols]
-
-    copies[3].wait()
+            block = slice(a * 256, a * 256 + 256)
+            acc[part, block, :] = mm(mates[block, 0:256], cold) - twice(nrow[block, :]) * crow[block, cols].astype(F32)
+
+    def near_rows(part, a, hot_rows):
+        block = slice(a * 256, a * 256 + 256)
+        change = acc[part, block, :] + mm(mates[block, 256:1024], hot_rows)
+        return (crow[block, part * 256 : part * 256 + 256].astype(F32) + change * twice(irow[block, :])).astype(BF)
+
     arrive(2)
     begin(0, ra2[...].reshape(256, 256))
     arrive(3)
-    begin(1, swap(rb2[...].reshape(256, 256)))
+    rowsb[...] = swap(rb2[...].reshape(256, 256))
+    begin(1, rowsb[...])
 
     arrive(5)
-    new_a = refresh(0, hot_a[...].reshape(768, 256))
-    gha[...] = mm(wt[256:1024, :], new_a).astype(BF).reshape(3, 4, 4, 16, 256)
+    for k in range(3):
+        gha[k] = near_rows(0, k + 1, hot_a[...].reshape(768, 256)).reshape(4, 4, 16, 256)
     for step in range(1, 4):
         to = (y + step) % 4
         start(12, gha.at[:, to], rha.at[y], zc, to * 4 + x)
     arrive(7)
-    new_b = refresh(1, hot_b[...].reshape(768, 256))
-    ghb[...] = mm(wt[256:1024, :], new_b).astype(BF).reshape(3, 4, 4, 16, 256)
+    for k in range(3):
+        ghb[k] = near_rows(1, k + 1, hot_b[...].reshape(768, 256)).reshape(4, 4, 16, 256)
     for step in range(1, 4):
         to = (x + step) % 4
         start(13, ghb.at[:, :, to], rhb.at[x], zc, y * 4 + to)
-    ga[...] = mm(wt[0:256, :], new_a).astype(BF).reshape(16, 16, 256)
+    ga[...] = near_rows(0, 0, hot_a[...].reshape(768, 256)).reshape(16, 16, 256)
     rga[g] = ga[g]
     along_g(10, ga, rga)
-    gb[...] = swap(mm(wt[0:256, :], new_b).astype(BF)).reshape(16, 16, 256)
+    gb[...] = swap(near_rows(1, 0, hot_b[...].reshape(768, 256))).reshape(16, 16, 256)
     rgb[zc] = gb[zc]
     along_zc(11, gb, rgb)
     rha[y] = gha[:, y]
     rhb[x] = ghb[:, :, x]
 
-    start(19, nvm, newc_hbm.at[:, half], zc + 1 - 2 * c, g)
-    own_copy = pltpu.make_async_copy(nvm, newc_hbm.at[:, half], local.at[5])
-    own_copy.start()
+    for t in range(4):
+        for a in range(8):
+            w[a * 128 : a * 128 + 128, t * 256 : t * 256 + 256] = onehot(iota((128, 256), 0) + a * 128 == lanes[t])
 
     arrive(12)
     h2a[...] = (rha[0] + rha[1]) + (rha[2] + rha[3])
@@ -303,6 +306,19 @@
     fb[...] = swap(rgb[...].reshape(256, 256)).reshape(16, 16, 256)
     rfb[g] = fb[g]
     along_g(15, fb, rfb)
+
+    for a in range(4):
+        lists = slice(a * 256, a * 256 + 256)
+        count = mm(w[lists, :], jnp.ones((1024, 128), BF))
+        scale = twice(1.0 / (prior_of[lists, :].astype(F32) + count))
+        for part, (cold, hot_rows) in enumerate(((ra2[...].reshape(256, 256), hot_a), (rowsb[...], hot_b))):
+            cols = slice(part * 256, part * 256 + 256)
+            old = cvm[lists, cols].astype(F32)
+            sums = mm(w[lists, 0:256], cold) + mm(w[lists, 256:1024], hot_rows[...].reshape(768, 256))
+            nvm[lists, cols] = (old + (sums - twice(count) * old) * scale).astype(BF)
+    start(19, nvm, newc_hbm.at[:, half], zc + 1 - 2 * c, g)
+    own_copy = pltpu.make_async_copy(nvm, newc_hbm.at[:, half], local.at[5])
+    own_copy.start()
 
     arrive(16)
     arrive(17)
@@ -349,12 +365,12 @@
     square, tall, plane = (16, 16, 256), (3, 4, 4, 16, 256), (4, 3, 16, 256)
     shapes = [
         (2, 16, 128), (16, 16, 128), (8, 2, 16, 256), square, square, square, square, square, square, square, tall, tall,
-        None, (1024, 1024), (1024, 1024), None, None, (1024, 512), (1024, 1024), (1024, 512), None,
+        None, (1024, 1024), (1024, 1024), (1024, 1024), (1024, 512), (1024, 128), (256, 256), None, None, (1024, 512), (1024, 1024), (1024, 512), None,
         square, square, tall, tall, square, square, (4, 3, 4, 16, 256), (4, 3, 4, 16, 256), square, square, square, square,
         (3, 4, 16, 256), (3, 4, 16, 256), plane, plane, (16, 16, 128), (16, 16, 128), (256, 256),
     ]
     others = [
-        pltpu.VMEM((4, 4, 16, 128), I32),
+        pltpu.VMEM((16, 16, 128), I32),
         pltpu.VMEM((1024, 128), F32),
         pltpu.VMEM((1024, 128), F32),
         pltpu.VMEM((2, 1024, 256), F32),
@@ -379,7 +395,7 @@
             pltpu.SemaphoreType.DMA((6,)),
         ],
         compiler_params=pltpu.CompilerParams(
-            collective_id=0, has_side_effects=True, vmem_limit_bytes=48 * 1024 * 1024
+            collective_id=0, has_side_effects=True, vmem_limit_bytes=58 * 1024 * 1024
         ),
         cost_estimate=pl.CostEstimate(flops=4_000_000_000, bytes_accessed=8_000_000, transcendentals=0),
     )(list_ids.reshape(1, 128), inserts, prior_counts.reshape(8, 128), centroids, rotation)

time: 56.7 us -> 53.7 us (0.947)
  local copies, waits for them, and re-layouts: 5.9 us -> 3.83 us
  Pallas kernels: 49.9 us -> 49.1 us
    unnamed x10 -> x4, local copies, waits for them, and re-layouts: 5.9 us -> 3.83 us
    pallas_call x1, Pallas kernels: 49.9 us -> 49.1 us  [per_device(): pl.pallas_call(kernel, out_shape=(jax.ShapeDtypeStruct(centroids.shape, B...]
where the time goes in v3:
time: 53.7 us; the launch traced here: 53.6 us
  Pallas kernels  49.1 us (91%)
  local copies, waits for them, and re-layouts  3.83 us (7%)
  between operations  0.65 us (1%)
    pallas_call x1, Pallas kernels, per_device(): pl.pallas_call(kernel, out_shape=(jax.ShapeDtypeStruct(centroids.shape, B...  49.1 us
    unnamed x4, local copies, waits for them, and re-layouts  3.83 us

profile of v3, /device:TPU:1, one launch (start us, length us, event | category | flops | bytes accessed | tf_op | source)
XLA Modules:
  0.0 53.6 jit_solution(7263817003912302328)
XLA Ops:
  0.6 49.1 %shard_map.68 = (bf16[1024,1024]{1,0:T(8,128)(2,1)}, bf16[128,1024]{1,0:T(8,128)(2,1)}) custom-call(s32[1,128]{1,0:T(1,128)} %bitcast.3, bf16[128,1024]{1,0:T(8,128)(2,1)} %x_hbm.1, s32[8,128]{1,0:T(8,128)} %bitcast.2, bf16[1024,1024]{1,0:T(8,128)(2,1)} %cent_hbm.1, bf16[1024,1024]{1,0:T(8,128)(2,1)} %rot_hbm.1), custom_call_target="tpu_custom_call" | custom-call | flops 4000000000 | bytes 8000000 | tf_op jit(solution)/shard_map/pallas_call | solution.py:382
  49.7 0.0 copy-start
  49.7 3.1 %copy.9 = bf16[1024,1024]{1,0:T(8,128)(2,1)} copy(bf16[1024,1024]{1,0:T(8,128)(2,1)} %get-tuple-element.4) | data formatting | bytes 4194304
  52.8 0.0 copy-done
  52.8 0.7 %copy.10 = bf16[128,1024]{1,0:T(8,128)(2,1)} copy(bf16[128,1024]{1,0:T(8,128)(2,1)S(1)} %copy-done) | data formatting | bytes 524288
Async XLA Ops:
  49.7 3.1 %copy-start = (bf16[128,1024]{1,0:T(8,128)(2,1)S(1)}, bf16[128,1024]{1,0:T(8,128)(2,1)}, u32[]{:S(2)}) copy-start(bf16[128,1024]{1,0:T(8,128)(2,1)} %get-tuple-element.5) | copy-start | bytes 786436

commit v4 on v3

--- a/solution.py
+++ b/solution.py
@@ -34,9 +34,9 @@
 
 def kernel(
     ids_hbm, x_hbm, prior_hbm, cent_hbm, rot_hbm, newc_hbm, out_ref,
-    ids_ref, x_ref, prior_ref, hbuf, hr, abuf, ra, bbuf, rb1, a2, ra2, b2, rb2, hot_a, hot_b, idb,
-    w, wt, mates, crow, prior_of, rowsb, nrow, irow, cvm, rvm, nvm, acc,
-    ga, gb, gha, ghb, rga, rgb, rha, rhb, fa, fb, rfa, rfb,
+    ids_ref, x_ref, prior_ref, hbuf, hr, bbuf, rb1, b2, rb2, hot_a, hot_b, idb,
+    w, wt, mates, crow, prior_of, cold, nrow, irow, cvm, rvm, nvm, acc,
+    gb, gha, ghb, rgb, rha, rhb, fb, rfb,
     h2a, h2b, rh2a, rh2b, ht, rht, perm, send, recv, local,
 ):
     c = lax.axis_index("replica")
@@ -49,12 +49,11 @@
 
 
     moved_by = {
-        0: [ra.at[pl.ds(0, 15)]], 20: [hr.at[pl.ds(0, 15)]], 1: [bbuf.at[pl.ds(0, 15)]], 2: [a2.at[pl.ds(0, 15)]], 3: [b2.at[pl.ds(0, 15)]],
+        20: [hr.at[pl.ds(0, 15)]], 1: [bbuf.at[pl.ds(0, 15)]], 3: [b2.at[pl.ds(0, 15)]], 8: [idb.at[pl.ds(0, 15)]],
         4: [hot_a.at[:, 0, pl.ds(0, 3)]], 5: [hot_a.at[:, pl.ds(0, 3)]], 6: [hot_b.at[:, 0, pl.ds(0, 3)]],
-        7: [hot_b.at[:, :, pl.ds(0, 3)]], 8: [idb.at[pl.ds(0, 15)]],
-        10: [ga.at[pl.ds(0, 15)]], 11: [gb.at[pl.ds(0, 15)]], 12: [gha.at[:, pl.ds(0, 3)]], 13: [ghb.at[:, :, pl.ds(0, 3)]],
-        14: [fa.at[pl.ds(0, 15)]], 15: [fb.at[pl.ds(0, 15)]], 16: [h2a.at[:, pl.ds(0, 3)]], 17: [h2b.at[:, pl.ds(0, 3)]],
-        18: [ht.at[pl.ds(0, 15)]], 19: [nvm],
+        7: [hot_b.at[:, :, pl.ds(0, 3)]], 11: [gb.at[pl.ds(0, 15)]], 12: [gha.at[:, pl.ds(0, 3)]],
+        13: [ghb.at[:, :, pl.ds(0, 3)]], 15: [fb.at[pl.ds(0, 15)]], 16: [h2a.at[:, pl.ds(0, 3)]],
+        17: [h2b.at[:, pl.ds(0, 3)]], 18: [ht.at[pl.ds(0, 15)]], 19: [nvm],
     }
     started, arrived = [], []
 
@@ -149,23 +148,11 @@
         to = (zc + step) % 16
         start(20, hbuf.at[to % 2], hr.at[zc], to, g)
 
-    r128 = iota((128, 128), 0)
-    pick = onehot(owner_at(r128 >> 4, r128 & 15) == cold_owner_row)
-    for cc in range(2):
-        block = mm(pick, x_ref[:, cc * 512 : cc * 512 + 256]).astype(BF)
-        abuf[:, cc] = block.reshape(8, 16, 256)
-    ra[zc] = abuf[z, c]
-
-    @pl.loop(1, 16)
-    def _(step):
-        to = (zc + step) % 16
-        start(0, abuf.at[to // 2, to % 2], ra.at[zc], to, g)
-
     r256 = iota((256, 128), 0)
     hit = owner_at((r256 & 15) >> 1, r256 >> 4) == cold_owner_row
-    part_b = mm(onehot(hit & ((r256 & 1) == 0)), x_ref[:, 256:512])
-    part_b = part_b + mm(onehot(hit & ((r256 & 1) == 1)), x_ref[:, 768:1024])
-    bbuf[...] = part_b.astype(BF).reshape(16, 16, 256)
+    rows_out = mm(onehot(hit & ((r256 & 1) == 0)), x_ref[:, 0:512])
+    rows_out = rows_out + mm(onehot(hit & ((r256 & 1) == 1)), x_ref[:, 512:1024])
+    bbuf[...] = rows_out.astype(BF).reshape(16, 16, 512)
     rb1[g] = bbuf[g]
     along_g(1, bbuf, rb1)
 
@@ -192,13 +179,8 @@
         start(4, hot_a.at[:, y, x], hot_a.at[:, y, x], zc, to)
         start(6, hot_b.at[:, y, x], hot_b.at[:, y, x], zc, ((y + step) % 4) * 4 + x)
 
-    arrive(0)
-    a2[...] = swap(ra[...].reshape(256, 256)).reshape(16, 16, 256)
-    ra2[g] = a2[g]
-    along_g(2, a2, ra2)
-
     arrive(1)
-    b2[...] = swap(rb1[...].reshape(256, 256)).reshape(16, 16, 256)
+    b2[...] = swap(rb1[...].reshape(256, 512)).reshape(16, 16, 512)
     rb2[zc] = b2[zc]
     along_zc(3, b2, rb2)
 
@@ -243,22 +225,21 @@
     def twice(rows128):
         return jnp.concatenate([rows128] * 2, axis=1)
 
-    def begin(part, cold):
+    def begin(part, cold_rows):
         cols = slice(part * 256, part * 256 + 256)
         for a in range(4):
             block = slice(a * 256, a * 256 + 256)
-            acc[part, block, :] = mm(mates[block, 0:256], cold) - twice(nrow[block, :]) * crow[block, cols].astype(F32)
+            acc[part, block, :] = mm(mates[block, 0:256], cold_rows) - twice(nrow[block, :]) * crow[block, cols].astype(F32)
 
     def near_rows(part, a, hot_rows):
         block = slice(a * 256, a * 256 + 256)
         change = acc[part, block, :] + mm(mates[block, 256:1024], hot_rows)
         return (crow[block, part * 256 : part * 256 + 256].astype(F32) + change * twice(irow[block, :])).astype(BF)
 
-    arrive(2)
-    begin(0, ra2[...].reshape(256, 256))
     arrive(3)
-    rowsb[...] = swap(rb2[...].reshape(256, 256))
-    begin(1, rowsb[...])
+    cold[...] = swap(rb2[...].reshape(256, 512))
+    begin(0, cold[:, 0:256])
+    begin(1, cold[:, 256:512])
 
     arrive(5)
     for k in range(3):
@@ -272,10 +253,9 @@
     for step in range(1, 4):
         to = (x + step) % 4
         start(13, ghb.at[:, :, to], rhb.at[x], zc, y * 4 + to)
-    ga[...] = near_rows(0, 0, hot_a[...].reshape(768, 256)).reshape(16, 16, 256)
-    rga[g] = ga[g]
-    along_g(10, ga, rga)
-    gb[...] = swap(near_rows(1, 0, hot_b[...].reshape(768, 256))).reshape(16, 16, 256)
+    for part, hot_part in enumerate((hot_a, hot_b)):
+        ready = swap(near_rows(part, 0, hot_part[...].reshape(768, 256)))
+        gb[:, :, part * 256 : part * 256 + 256] = ready.reshape(16, 16, 256)
     rgb[zc] = gb[zc]
     along_zc(11, gb, rgb)
     rha[y] = gha[:, y]
@@ -284,6 +264,19 @@
     for t in range(4):
         for a in range(8):
             w[a * 128 : a * 128 + 128, t * 256 : t * 256 + 256] = onehot(iota((128, 256), 0) + a * 128 == lanes[t])
+
+    for a in range(4):
+        lists = slice(a * 256, a * 256 + 256)
+        count = mm(w[lists, :], jnp.ones((1024, 128), BF))
+        scale = twice(1.0 / (prior_of[lists, :].astype(F32) + count))
+        for part, hot_rows in enumerate((hot_a, hot_b)):
+            cols = slice(part * 256, part * 256 + 256)
+            old = cvm[lists, cols].astype(F32)
+            sums = mm(w[lists, 0:256], cold[:, cols]) + mm(w[lists, 256:1024], hot_rows[...].reshape(768, 256))
+            nvm[lists, cols] = (old + (sums - twice(count) * old) * scale).astype(BF)
+    start(19, nvm, newc_hbm.at[:, half], zc + 1 - 2 * c, g)
+    own_copy = pltpu.make_async_copy(nvm, newc_hbm.at[:, half], local.at[5])
+    own_copy.start()
 
     arrive(12)
     h2a[...] = (rha[0] + rha[1]) + (rha[2] + rha[3])
@@ -298,27 +291,10 @@
         start(17, h2b.at[:, to], rh2b.at[y], zc, to * 4 + x)
     rh2b[y] = h2b[:, y]
 
-    arrive(10)
-    fa[...] = swap(rga[...].reshape(256, 256)).reshape(16, 16, 256)
-    rfa[zc] = fa[zc]
-    along_zc(14, fa, rfa)
     arrive(11)
-    fb[...] = swap(rgb[...].reshape(256, 256)).reshape(16, 16, 256)
+    fb[...] = swap(rgb[...].reshape(256, 512)).reshape(16, 16, 512)
     rfb[g] = fb[g]
     along_g(15, fb, rfb)
-
-    for a in range(4):
-        lists = slice(a * 256, a * 256 + 256)
-        count = mm(w[lists, :], jnp.ones((1024, 128), BF))
-        scale = twice(1.0 / (prior_of[lists, :].astype(F32) + count))
-        for part, (cold, hot_rows) in enumerate(((ra2[...].reshape(256, 256), hot_a), (rowsb[...], hot_b))):
-            cols = slice(part * 256, part * 256 + 256)
-            old = cvm[lists, cols].astype(F32)
-            sums = mm(w[lists, 0:256], cold) + mm(w[lists, 256:1024], hot_rows[...].reshape(768, 256))
-            nvm[lists, cols] = (old + (sums - twice(count) * old) * scale).astype(BF)
-    start(19, nvm, newc_hbm.at[:, half], zc + 1 - 2 * c, g)
-    own_copy = pltpu.make_async_copy(nvm, newc_hbm.at[:, half], local.at[5])
-    own_copy.start()
 
     arrive(16)
     arrive(17)
@@ -332,14 +308,9 @@
     along_zc(18, ht, rht)
 
     lane = iota((128, 256), 1)
-    hit_a = owner_at(lane >> 5, lane & 15) == cold_owner_col
-    hit_b = owner_at((lane & 15) >> 1, lane >> 4) == cold_owner_col
-    arrive(14)
+    hit_col = owner_at((lane & 15) >> 1, lane >> 4) == cold_owner_col
     arrive(15)
-    picked = []
-    for cc in range(2):
-        picked.append(mm(onehot(hit_a & ((lane >> 4) & 1 == cc)), rfa[...].reshape(256, 256)))
-        picked.append(mm(onehot(hit_b & (lane & 1 == cc)), rfb[...].reshape(256, 256)))
+    picked = [mm(onehot(hit_col & (lane & 1 == cc)), rfb[...].reshape(256, 512)) for cc in range(2)]
     arrive(18)
     tile_lane = iota((128, 16), 1)
     tiles = []
@@ -361,12 +332,28 @@
     finish()
 
 
+def hand_over(newc_from, rotated_from, newc_to, rotated_to, newc_here, rotated_here, sem_in, sem_out):
+    moves = [(rotated_from, rotated_here, rotated_to)]
+    for n in range(8):
+        rows = pl.ds(n * 128, 128)
+        moves.append((newc_from.at[rows], newc_here.at[rows], newc_to.at[rows]))
+    reads = [pltpu.make_async_copy(src, mid, sem_in.at[n]) for n, (src, mid, _) in enumerate(moves)]
+    writes = [pltpu.make_async_copy(mid, dst, sem_out.at[n]) for n, (_, mid, dst) in enumerate(moves)]
+    for read in reads:
+        read.start()
+    for read, write in zip(reads, writes):
+        read.wait()
+        write.start()
+    for write in writes:
+        write.wait()
+
+
 def per_device(inserts, list_ids, centroids, prior_counts, rotation):
-    square, tall, plane = (16, 16, 256), (3, 4, 4, 16, 256), (4, 3, 16, 256)
+    square, tall, plane = (16, 16, 512), (3, 4, 4, 16, 256), (4, 3, 16, 256)
     shapes = [
-        (2, 16, 128), (16, 16, 128), (8, 2, 16, 256), square, square, square, square, square, square, square, tall, tall,
-        None, (1024, 1024), (1024, 1024), (1024, 1024), (1024, 512), (1024, 128), (256, 256), None, None, (1024, 512), (1024, 1024), (1024, 512), None,
-        square, square, tall, tall, square, square, (4, 3, 4, 16, 256), (4, 3, 4, 16, 256), square, square, square, square,
+        (2, 16, 128), (16, 16, 128), square, square, square, square, tall, tall,
+        None, (1024, 1024), (1024, 1024), (1024, 1024), (1024, 512), (1024, 128), (256, 512), None, None, (1024, 512), (1024, 1024), (1024, 512), None,
+        square, tall, tall, square, (4, 3, 4, 16, 256), (4, 3, 4, 16, 256), square, square,
         (3, 4, 16, 256), (3, 4, 16, 256), plane, plane, (16, 16, 128), (16, 16, 128), (256, 256),
     ]
     others = [
@@ -379,12 +366,10 @@
     given = [pltpu.VMEM((1, 128), I32), pltpu.VMEM(inserts.shape, BF), pltpu.VMEM((8, 128), I32)]
     vmem = pl.BlockSpec(memory_space=pltpu.VMEM)
     anywhere = pl.BlockSpec(memory_space=pl.ANY)
-    return pl.pallas_call(
+    results = (jax.ShapeDtypeStruct(centroids.shape, BF), jax.ShapeDtypeStruct(inserts.shape, BF))
+    made = pl.pallas_call(
         kernel,
-        out_shape=(
-            jax.ShapeDtypeStruct(centroids.shape, BF),
-            jax.ShapeDtypeStruct(inserts.shape, BF),
-        ),
+        out_shape=results,
         in_specs=[pl.BlockSpec(memory_space=pltpu.HBM)] * 5,
         out_specs=(anywhere, vmem),
         scratch_shapes=given
@@ -399,6 +384,19 @@
         ),
         cost_estimate=pl.CostEstimate(flops=4_000_000_000, bytes_accessed=8_000_000, transcendentals=0),
     )(list_ids.reshape(1, 128), inserts, prior_counts.reshape(8, 128), centroids, rotation)
+    hbm = pl.BlockSpec(memory_space=pltpu.HBM)
+    return pl.pallas_call(
+        hand_over,
+        out_shape=results,
+        in_specs=[anywhere] * 2,
+        out_specs=(hbm, hbm),
+        scratch_shapes=[
+            pltpu.VMEM(centroids.shape, BF),
+            pltpu.VMEM(inserts.shape, BF),
+            pltpu.SemaphoreType.DMA((9,)),
+            pltpu.SemaphoreType.DMA((9,)),
+        ],
+    )(*made)
 
 
 def solution(mesh):

time: 53.7 us -> 49.5 us (0.922)
  local copies, waits for them, and re-layouts: 3.83 us -> 0 us
    unnamed x4 -> x0, local copies, waits for them, and re-layouts: 3.83 us -> none
    pallas_call x1 -> x2, Pallas kernels: 49.1 us -> 48.7 us  [the longest x1 46.2 us: per_device(): pl.pallas_call(kernel, out_shape=results, in_specs=[pl.BlockSpec(memory_s...]
where the time goes in v4:
time: 49.5 us; the launch traced here: 49.4 us
  Pallas kernels  48.7 us (98%)
  between operations  0.64 us (1%)
    pallas_call x1, Pallas kernels, per_device(): pl.pallas_call(kernel, out_shape=results, in_specs=[pl.BlockSpec(memory_s...  46.2 us
    pallas_call x1, Pallas kernels, per_device(): pl.pallas_call(hand_over, out_shape=results, in_specs=[anywhere] * 2, out...  2.5 us

profile of v4, /device:TPU:1, one launch (start us, length us, event | category | flops | bytes accessed | tf_op | source)
XLA Modules:
  0.0 49.4 jit_solution(14013215876671396100)
XLA Ops:
  0.6 46.2 %shard_map.68 = (bf16[1024,1024]{1,0:T(8,128)(2,1)}, bf16[128,1024]{1,0:T(8,128)(2,1)}) custom-call(s32[1,128]{1,0:T(1,128)} %bitcast.3, bf16[128,1024]{1,0:T(8,128)(2,1)} %x_hbm.1, s32[8,128]{1,0:T(8,128)} %bitcast.2, bf16[1024,1024]{1,0:T(8,128)(2,1)} %cent_hbm.1, bf16[1024,1024]{1,0:T(8,128)(2,1)} %rot_hbm.1), custom_call_target="tpu_custom_call" | custom-call | flops 4000000000 | bytes 8000000 | tf_op jit(solution)/shard_map/pallas_call | solution.py:370
  46.9 2.5 %shard_map.69 = (bf16[1024,1024]{1,0:T(8,128)(2,1)}, bf16[128,1024]{1,0:T(8,128)(2,1)}) custom-call(bf16[1024,1024]{1,0:T(8,128)(2,1)} %get-tuple-element.4.newc_from, bf16[128,1024]{1,0:T(8,128)(2,1)} %get-tuple-element.5.rotated_from), custom_call_target="tpu_custom_call" | custom-call | tf_op jit(solution)/shard_map/pallas_call | solution.py:388

commit v5 on v4

--- a/solution.py
+++ b/solution.py
@@ -33,11 +33,11 @@
 
 
 def kernel(
-    ids_hbm, x_hbm, prior_hbm, cent_hbm, rot_hbm, newc_hbm, out_ref,
+    ids_hbm, x_hbm, prior_hbm, cent_hbm, newc_hbm, rfb, rht,
     ids_ref, x_ref, prior_ref, hbuf, hr, bbuf, rb1, b2, rb2, hot_a, hot_b, idb,
-    w, wt, mates, crow, prior_of, cold, nrow, irow, cvm, rvm, nvm, acc,
-    gb, gha, ghb, rgb, rha, rhb, fb, rfb,
-    h2a, h2b, rh2a, rh2b, ht, rht, perm, send, recv, local,
+    w, wt, mates, crow, prior_of, cold, nrow, irow, cvm, nvm, acc,
+    gb, gha, ghb, rgb, rha, rhb, fb,
+    h2a, h2b, rh2a, rh2b, ht, perm, send, recv, local,
 ):
     c = lax.axis_index("replica")
     li = lax.axis_index("lists")
@@ -102,7 +102,7 @@
     copies = [
         pltpu.make_async_copy(src, dst, local.at[n])
         for n, (src, dst) in enumerate(
-            ((ids_hbm, ids_ref), (x_hbm, x_ref), (prior_hbm, prior_ref), (cent_hbm.at[:, half], cvm), (rot_hbm, rvm))
+            ((ids_hbm, ids_ref), (x_hbm, x_ref), (prior_hbm, prior_ref), (cent_hbm.at[:, half], cvm))
         )
     ]
     for copy in copies:
@@ -115,11 +115,8 @@
     owner_col = jnp.sum(jnp.where(eye, owner_row, 0), axis=1, keepdims=True)
     same = jnp.where(owner_col == owner_row, 1.0, 0.0)
     earlier = jnp.where(iota((128, 128), 0) < iota((128, 128), 1), same, 0.0)
-    later = jnp.where(iota((128, 128), 1) < iota((128, 128), 0), same, 0.0)
     rank_row = jnp.sum(earlier, axis=0, keepdims=True)
-    rank_col = jnp.sum(later, axis=1, keepdims=True)
     cold_owner_row = jnp.where(rank_row > 0.5, -1, owner_row)
-    cold_owner_col = jnp.where(rank_col > 0.5, -1, owner_col)
 
     tile_row = iota((16, 128), 0)
     info = jnp.where(tile_row == 12, owner_row, 0)
@@ -140,20 +137,20 @@
     def swap(rows):
         return mm(perm[...], rows).astype(BF)
 
-    hr[zc] = hbuf[c]
-    pl.semaphore_wait(barrier, 30)
-
-    @pl.loop(1, 16)
-    def _(step):
-        to = (zc + step) % 16
-        start(20, hbuf.at[to % 2], hr.at[zc], to, g)
-
     r256 = iota((256, 128), 0)
     hit = owner_at((r256 & 15) >> 1, r256 >> 4) == cold_owner_row
     rows_out = mm(onehot(hit & ((r256 & 1) == 0)), x_ref[:, 0:512])
     rows_out = rows_out + mm(onehot(hit & ((r256 & 1) == 1)), x_ref[:, 512:1024])
     bbuf[...] = rows_out.astype(BF).reshape(16, 16, 512)
     rb1[g] = bbuf[g]
+    hr[zc] = hbuf[c]
+    pl.semaphore_wait(barrier, 30)
+
+    @pl.loop(1, 16)
+    def _(step):
+        to = (zc + step) % 16
+        start(20, hbuf.at[to % 2], hr.at[zc], to, g)
+
     along_g(1, bbuf, rb1)
 
     copies[2].wait()
@@ -167,17 +164,16 @@
     hot = hot_rows.astype(BF)
     for j, (ref, low) in enumerate(((hot_a, 0), (hot_a, 128), (hot_b, 0), (hot_b, 128))):
         ref[:, y, x, :, low : low + 128] = hot[j * 48 : j * 48 + 48].reshape(3, 16, 128)
+    for step in range(1, 4):
+        to = y * 4 + (x + step) % 4
+        start(4, hot_a.at[:, y, x], hot_a.at[:, y, x], zc, to)
+        start(6, hot_b.at[:, y, x], hot_b.at[:, y, x], zc, ((y + step) % 4) * 4 + x)
     got = hot_rows[192:256].astype(I32)
     idb[g] = (got[48:64] << 17) + (got[0:16] << 10) + (got[16:32] << 5) + got[32:48]
 
     @pl.loop(1, 16)
     def _(step):
         start(8, idb.at[g], idb.at[g], zc, (g + step) % 16)
-
-    for step in range(1, 4):
-        to = y * 4 + (x + step) % 4
-        start(4, hot_a.at[:, y, x], hot_a.at[:, y, x], zc, to)
-        start(6, hot_b.at[:, y, x], hot_b.at[:, y, x], zc, ((y + step) % 4) * 4 + x)
 
     arrive(1)
     b2[...] = swap(rb1[...].reshape(256, 512)).reshape(16, 16, 512)
@@ -293,7 +289,8 @@
 
     arrive(11)
     fb[...] = swap(rgb[...].reshape(256, 512)).reshape(16, 16, 512)
-    rfb[g] = fb[g]
+    own_fb = pltpu.make_async_copy(fb.at[g], rfb.at[g], local.at[4])
+    own_fb.start()
     along_g(15, fb, rfb)
 
     arrive(16)
@@ -304,14 +301,42 @@
         [back_a[:, :128], back_a[:, 128:], back_b[:, :128], back_b[:, 128:], jnp.zeros((64, 128), BF)], axis=0
     )
     ht[...] = swap(back).reshape(16, 16, 128)
-    rht[zc] = ht[zc]
+    own_ht = pltpu.make_async_copy(ht.at[zc], rht.at[zc], local.at[6])
+    own_ht.start()
     along_zc(18, ht, rht)
 
+    own_fb.wait()
+    own_ht.wait()
+    own_copy.wait()
+    finish()
+
+
+def finish_rows(
+    ids_hbm, x_hbm, rot_hbm, newc_from, rfb_from, rht_from, newc_to, rotated_to,
+    ids_ref, x_ref, rvm, newc_here, rfb, rht, rotated, sem_in, sem_out,
+):
+    given = ((ids_hbm, ids_ref), (rfb_from, rfb), (rht_from, rht), (x_hbm, x_ref), (rot_hbm, rvm))
+    reads = [pltpu.make_async_copy(src, dst, sem_in.at[n]) for n, (src, dst) in enumerate(given)]
+    for read in reads:
+        read.start()
+    halves = [pl.ds(n * 256, 256) for n in range(4)]
+    table_in = [pltpu.make_async_copy(newc_from.at[rows], newc_here.at[rows], sem_in.at[5 + n]) for n, rows in enumerate(halves)]
+    table_out = [pltpu.make_async_copy(newc_here.at[rows], newc_to.at[rows], sem_out.at[n]) for n, rows in enumerate(halves)]
+    for copy in table_in:
+        copy.start()
+
+    reads[0].wait()
+    owner_row = ids_ref[...] >> 10
+    eye = iota((128, 128), 0) == iota((128, 128), 1)
+    owner_col = jnp.sum(jnp.where(eye, owner_row, 0), axis=1, keepdims=True)
+    same = jnp.where(owner_col == owner_row, 1.0, 0.0)
+    later = jnp.where(iota((128, 128), 1) < iota((128, 128), 0), same, 0.0)
+    rank_col = jnp.sum(later, axis=1, keepdims=True)
     lane = iota((128, 256), 1)
-    hit_col = owner_at((lane & 15) >> 1, lane >> 4) == cold_owner_col
-    arrive(15)
+    hit_col = owner_at((lane & 15) >> 1, lane >> 4) == jnp.where(rank_col > 0.5, -1, owner_col)
+    reads[1].wait()
     picked = [mm(onehot(hit_col & (lane & 1 == cc)), rfb[...].reshape(256, 512)) for cc in range(2)]
-    arrive(18)
+    reads[2].wait()
     tile_lane = iota((128, 16), 1)
     tiles = []
     for cc in range(2):
@@ -322,39 +347,29 @@
             match = (tile_lane >= j * 3) & (tile_lane < j * 3 + 3) & ((tile_lane - (j * 3 - 1)).astype(F32) == rank_col)
             tiles.append(mm(onehot(match), tile))
     near = jnp.concatenate(picked, axis=1) + jnp.concatenate(tiles, axis=1)
+    reads[3].wait()
     residual = (x_ref[...].astype(F32) - near).astype(BF)
-    copies[4].wait()
+    reads[4].wait()
+    for copy_in, copy_out in zip(table_in, table_out):
+        copy_in.wait()
+        copy_out.start()
+    sent = []
     for a in range(4):
         cols = slice(a * 256, a * 256 + 256)
-        out_ref[:, cols] = mm(residual, rvm[:, cols]).astype(BF)
-
-    own_copy.wait()
-    finish()
-
-
-def hand_over(newc_from, rotated_from, newc_to, rotated_to, newc_here, rotated_here, sem_in, sem_out):
-    moves = [(rotated_from, rotated_here, rotated_to)]
-    for n in range(8):
-        rows = pl.ds(n * 128, 128)
-        moves.append((newc_from.at[rows], newc_here.at[rows], newc_to.at[rows]))
-    reads = [pltpu.make_async_copy(src, mid, sem_in.at[n]) for n, (src, mid, _) in enumerate(moves)]
-    writes = [pltpu.make_async_copy(mid, dst, sem_out.at[n]) for n, (_, mid, dst) in enumerate(moves)]
-    for read in reads:
-        read.start()
-    for read, write in zip(reads, writes):
-        read.wait()
-        write.start()
-    for write in writes:
-        write.wait()
+        rotated[:, cols] = mm(residual, rvm[:, cols]).astype(BF)
+        sent.append(pltpu.make_async_copy(rotated.at[:, pl.ds(a * 256, 256)], rotated_to.at[:, pl.ds(a * 256, 256)], sem_out.at[4 + a]))
+        sent[a].start()
+    for copy in table_out + sent:
+        copy.wait()
 
 
 def per_device(inserts, list_ids, centroids, prior_counts, rotation):
     square, tall, plane = (16, 16, 512), (3, 4, 4, 16, 256), (4, 3, 16, 256)
     shapes = [
         (2, 16, 128), (16, 16, 128), square, square, square, square, tall, tall,
-        None, (1024, 1024), (1024, 1024), (1024, 1024), (1024, 512), (1024, 128), (256, 512), None, None, (1024, 512), (1024, 1024), (1024, 512), None,
-        square, tall, tall, square, (4, 3, 4, 16, 256), (4, 3, 4, 16, 256), square, square,
-        (3, 4, 16, 256), (3, 4, 16, 256), plane, plane, (16, 16, 128), (16, 16, 128), (256, 256),
+        None, (1024, 1024), (1024, 1024), (1024, 1024), (1024, 512), (1024, 128), (256, 512), None, None, (1024, 512), (1024, 512), None,
+        square, tall, tall, square, (4, 3, 4, 16, 256), (4, 3, 4, 16, 256), square,
+        (3, 4, 16, 256), (3, 4, 16, 256), plane, plane, (16, 16, 128), (256, 256),
     ]
     others = [
         pltpu.VMEM((16, 16, 128), I32),
@@ -364,39 +379,46 @@
     ]
     scratch = [pltpu.VMEM(shape, BF) if shape else others.pop(0) for shape in shapes]
     given = [pltpu.VMEM((1, 128), I32), pltpu.VMEM(inserts.shape, BF), pltpu.VMEM((8, 128), I32)]
-    vmem = pl.BlockSpec(memory_space=pltpu.VMEM)
-    anywhere = pl.BlockSpec(memory_space=pl.ANY)
-    results = (jax.ShapeDtypeStruct(centroids.shape, BF), jax.ShapeDtypeStruct(inserts.shape, BF))
+    anywhere, hbm = pl.BlockSpec(memory_space=pl.ANY), pl.BlockSpec(memory_space=pltpu.HBM)
+    ids = list_ids.reshape(1, 128)
+    back_rows, back_tiles = jax.ShapeDtypeStruct(square, BF), jax.ShapeDtypeStruct((16, 16, 128), BF)
+    table, rows_of = jax.ShapeDtypeStruct(centroids.shape, BF), jax.ShapeDtypeStruct(inserts.shape, BF)
     made = pl.pallas_call(
         kernel,
-        out_shape=results,
-        in_specs=[pl.BlockSpec(memory_space=pltpu.HBM)] * 5,
-        out_specs=(anywhere, vmem),
+        out_shape=(table, back_rows, back_tiles),
+        in_specs=[hbm] * 4,
+        out_specs=(anywhere,) * 3,
         scratch_shapes=given
         + scratch
         + [
             pltpu.SemaphoreType.DMA((STAGES,)),
             pltpu.SemaphoreType.DMA((STAGES,)),
-            pltpu.SemaphoreType.DMA((6,)),
+            pltpu.SemaphoreType.DMA((7,)),
         ],
         compiler_params=pltpu.CompilerParams(
             collective_id=0, has_side_effects=True, vmem_limit_bytes=58 * 1024 * 1024
         ),
         cost_estimate=pl.CostEstimate(flops=4_000_000_000, bytes_accessed=8_000_000, transcendentals=0),
-    )(list_ids.reshape(1, 128), inserts, prior_counts.reshape(8, 128), centroids, rotation)
-    hbm = pl.BlockSpec(memory_space=pltpu.HBM)
+    )(ids, inserts, prior_counts.reshape(8, 128), centroids)
     return pl.pallas_call(
-        hand_over,
-        out_shape=results,
-        in_specs=[anywhere] * 2,
+        finish_rows,
+        out_shape=(table, rows_of),
+        in_specs=[anywhere] * 6,
         out_specs=(hbm, hbm),
         scratch_shapes=[
+            pltpu.VMEM((1, 128), I32),
+            pltpu.VMEM(inserts.shape, BF),
+            pltpu.VMEM(rotation.shape, BF),
             pltpu.VMEM(centroids.shape, BF),
+            pltpu.VMEM(square, BF),
+            pltpu.VMEM((16, 16, 128), BF),
             pltpu.VMEM(inserts.shape, BF),
             pltpu.SemaphoreType.DMA((9,)),
-            pltpu.SemaphoreType.DMA((9,)),
+            pltpu.SemaphoreType.DMA((8,)),
         ],
-    )(*made)
+        compiler_params=pltpu.CompilerParams(vmem_limit_bytes=58 * 1024 * 1024),
+        cost_estimate=pl.CostEstimate(flops=400_000_000, bytes_accessed=9_000_000, transcendentals=0),
+    )(ids, inserts, rotation, *made)
 
 
 def solution(mesh):

time: 49.5 us -> 48.2 us (0.974)
  Pallas kernels: 48.7 us -> 47.4 us
    pallas_call x2, Pallas kernels: 48.7 us -> 47.4 us  [the longest x1 43.8 us: per_device(): pl.pallas_call(kernel, out_shape=(table, back_rows, back_tiles), in_specs...]
where the time goes in v5:
time: 48.2 us; the launch traced here: 48.1 us
  Pallas kernels  47.4 us (98%)
  between operations  0.64 us (1%)
    pallas_call x1, Pallas kernels, per_device(): pl.pallas_call(kernel, out_shape=(table, back_rows, back_tiles), in_specs...  43.8 us
    pallas_call x1, Pallas kernels, per_device(): pl.pallas_call(finish_rows, out_shape=(table, rows_of), in_specs=[anywher...  3.61 us

profile of v5, /device:TPU:1, one launch (start us, length us, event | category | flops | bytes accessed | tf_op | source)
XLA Modules:
  0.0 48.1 jit_solution(7852491095805698387)
XLA Ops:
  0.6 43.8 %shard_map.68 = (bf16[1024,1024]{1,0:T(8,128)(2,1)}, bf16[16,16,512]{2,1,0:T(8,128)(2,1)}, bf16[16,16,128]{2,1,0:T(8,128)(2,1)}) custom-call(s32[1,128]{1,0:T(1,128)} %bitcast.2, bf16[128,1024]{1,0:T(8,128)(2,1)} %x_hbm.3, s32[8,128]{1,0:T(8,128)} %bitcast.4, bf16[1024,1024]{1,0:T(8,128)(2,1)} %cent_hbm.1), custom_call_target="tpu_custom_call" | custom-call | flops 4000000000 | bytes 8000000 | tf_op jit(solution)/shard_map/pallas_call | solution.py:386
  44.5 3.6 %shard_map.69 = (bf16[1024,1024]{1,0:T(8,128)(2,1)}, bf16[128,1024]{1,0:T(8,128)(2,1)}) custom-call(s32[1,128]{1,0:T(1,128)} %bitcast.3, bf16[128,1024]{1,0:T(8,128)(2,1)} %x_hbm.3, bf16[1024,1024]{1,0:T(8,128)(2,1)} %rot_hbm.1, bf16[1024,1024]{1,0:T(8,128)(2,1)} %get-tuple-element.5.newc_from, bf16[16,16,512]{2,1,0:T(8,128)(2,1)} %get-tuple-element.6.rfb_from, ...), custom_call_target="tpu_custom_call" | custom-call | flops 400000000 | bytes 9000000 | tf_op jit(solution)/shard_map/pallas_call | solution.py:403

commit v6 on v5

--- a/solution.py
+++ b/solution.py
@@ -9,7 +9,7 @@
 BF = jnp.bfloat16
 F32 = jnp.float32
 I32 = jnp.int32
-STAGES = 21
+STAGES = 25
 
 
 def mm(a, b):
@@ -50,9 +50,9 @@
 
     moved_by = {
         20: [hr.at[pl.ds(0, 15)]], 1: [bbuf.at[pl.ds(0, 15)]], 3: [b2.at[pl.ds(0, 15)]], 8: [idb.at[pl.ds(0, 15)]],
-        4: [hot_a.at[:, 0, pl.ds(0, 3)]], 5: [hot_a.at[:, pl.ds(0, 3)]], 6: [hot_b.at[:, 0, pl.ds(0, 3)]],
-        7: [hot_b.at[:, :, pl.ds(0, 3)]], 11: [gb.at[pl.ds(0, 15)]], 12: [gha.at[:, pl.ds(0, 3)]],
-        13: [ghb.at[:, :, pl.ds(0, 3)]], 15: [fb.at[pl.ds(0, 15)]], 16: [h2a.at[:, pl.ds(0, 3)]],
+        4: [hot_a.at[:, 0, pl.ds(0, 3)]], 5: [hot_a.at[:, pl.ds(0, 3), pl.ds(0, 3)]], 6: [hot_b.at[:, 0, pl.ds(0, 3)]],
+        7: [hot_b.at[:, pl.ds(0, 3), pl.ds(0, 3)]], 21: [hot_a.at[:, 0, pl.ds(0, 3)]], 22: [hot_b.at[:, 0, pl.ds(0, 3)]], 11: [gb.at[pl.ds(0, 15)]], 12: [gha.at[:, pl.ds(0, 3), pl.ds(0, 3)]], 23: [gha.at[:, 0, pl.ds(0, 3)]],
+        13: [ghb.at[:, pl.ds(0, 3), pl.ds(0, 3)]], 24: [ghb.at[:, 0, pl.ds(0, 3)]], 15: [fb.at[pl.ds(0, 15)]], 16: [h2a.at[:, pl.ds(0, 3)]],
         17: [h2b.at[:, pl.ds(0, 3)]], 18: [ht.at[pl.ds(0, 15)]], 19: [nvm],
     }
     started, arrived = [], []
@@ -168,6 +168,9 @@
         to = y * 4 + (x + step) % 4
         start(4, hot_a.at[:, y, x], hot_a.at[:, y, x], zc, to)
         start(6, hot_b.at[:, y, x], hot_b.at[:, y, x], zc, ((y + step) % 4) * 4 + x)
+    for step in range(1, 4):
+        start(21, hot_a.at[:, y, x], hot_a.at[:, y, x], zc, ((y + step) % 4) * 4 + x)
+        start(22, hot_b.at[:, y, x], hot_b.at[:, y, x], zc, y * 4 + (x + step) % 4)
     got = hot_rows[192:256].astype(I32)
     idb[g] = (got[48:64] << 17) + (got[0:16] << 10) + (got[16:32] << 5) + got[32:48]
 
@@ -184,8 +187,10 @@
     arrive(6)
     for step in range(1, 4):
         to = ((y + step) % 4) * 4 + x
-        start(5, hot_a.at[:, y], hot_a.at[:, y], zc, to)
-        start(7, hot_b.at[:, :, x], hot_b.at[:, :, x], zc, y * 4 + (x + step) % 4)
+        for other in range(1, 4):
+            xx, yy = (x + other) % 4, (y + other) % 4
+            start(5, hot_a.at[:, y, xx], hot_a.at[:, y, xx], zc, to)
+            start(7, hot_b.at[:, yy, x], hot_b.at[:, yy, x], zc, y * 4 + (x + step) % 4)
 
     arrive(8)
     code = idb[...].reshape(256, 128)
@@ -238,17 +243,26 @@
     begin(1, cold[:, 256:512])
 
     arrive(5)
+    arrive(21)
     for k in range(3):
         gha[k] = near_rows(0, k + 1, hot_a[...].reshape(768, 256)).reshape(4, 4, 16, 256)
     for step in range(1, 4):
         to = (y + step) % 4
-        start(12, gha.at[:, to], rha.at[y], zc, to * 4 + x)
+        for other in range(1, 4):
+            xx = (x + other) % 4
+            start(12, gha.at[:, to, xx], rha.at[y, :, xx], zc, to * 4 + x)
     arrive(7)
+    arrive(22)
     for k in range(3):
         ghb[k] = near_rows(1, k + 1, hot_b[...].reshape(768, 256)).reshape(4, 4, 16, 256)
     for step in range(1, 4):
         to = (x + step) % 4
-        start(13, ghb.at[:, :, to], rhb.at[x], zc, y * 4 + to)
+        for other in range(1, 4):
+            yy = (y + other) % 4
+            start(13, ghb.at[:, yy, to], rhb.at[x, :, yy], zc, y * 4 + to)
+    for step in range(1, 4):
+        start(23, gha.at[:, (y + step) % 4, x], rha.at[y, :, x], zc, ((y + step) % 4) * 4 + x)
+        start(24, ghb.at[:, y, (x + step) % 4], rhb.at[x, :, y], zc, y * 4 + (x + step) % 4)
     for part, hot_part in enumerate((hot_a, hot_b)):
         ready = swap(near_rows(part, 0, hot_part[...].reshape(768, 256)))
         gb[:, :, part * 256 : part * 256 + 256] = ready.reshape(16, 16, 256)
@@ -274,18 +288,23 @@
     own_copy = pltpu.make_async_copy(nvm, newc_hbm.at[:, half], local.at[5])
     own_copy.start()
 
+    def gathered(ref, at):
+        return (ref[0, :, at] + ref[1, :, at]) + (ref[2, :, at] + ref[3, :, at])
+
     arrive(12)
-    h2a[...] = (rha[0] + rha[1]) + (rha[2] + rha[3])
     for step in range(1, 4):
         to = (x + step) % 4
+        h2a[:, to] = gathered(rha, to)
         start(16, h2a.at[:, to], rh2a.at[x], zc, y * 4 + to)
-    rh2a[x] = h2a[:, x]
     arrive(13)
-    h2b[...] = (rhb[0] + rhb[1]) + (rhb[2] + rhb[3])
     for step in range(1, 4):
         to = (y + step) % 4
+        h2b[:, to] = gathered(rhb, to)
         start(17, h2b.at[:, to], rh2b.at[y], zc, to * 4 + x)
-    rh2b[y] = h2b[:, y]
+    arrive(23)
+    rh2a[x] = gathered(rha, x)
+    arrive(24)
+    rh2b[y] = gathered(rhb, y)
 
     arrive(11)
     fb[...] = swap(rgb[...].reshape(256, 512)).reshape(16, 16, 512)

time: 48.2 us -> 48.1 us (level)
  no operation moved by 1% of the time
where the time goes in v6:
time: 48.1 us; the launch traced here: 48 us
  Pallas kernels  47.4 us (99%)
  between operations  0.64 us (1%)
    pallas_call x1, Pallas kernels, per_device(): pl.pallas_call(kernel, out_shape=(table, back_rows, back_tiles), in_specs...  43.8 us
    pallas_call x1, Pallas kernels, per_device(): pl.pallas_call(finish_rows, out_shape=(table, rows_of), in_specs=[anywher...  3.61 us

profile of v6, /device:TPU:1, one launch (start us, length us, event | category | flops | bytes accessed | tf_op | source)
XLA Modules:
  0.0 48.0 jit_solution(12497709799413437597)
XLA Ops:
  0.6 43.8 %shard_map.68 = (bf16[1024,1024]{1,0:T(8,128)(2,1)}, bf16[16,16,512]{2,1,0:T(8,128)(2,1)}, bf16[16,16,128]{2,1,0:T(8,128)(2,1)}) custom-call(s32[1,128]{1,0:T(1,128)} %bitcast.2, bf16[128,1024]{1,0:T(8,128)(2,1)} %x_hbm.3, s32[8,128]{1,0:T(8,128)} %bitcast.4, bf16[1024,1024]{1,0:T(8,128)(2,1)} %cent_hbm.1), custom_call_target="tpu_custom_call" | custom-call | flops 4000000000 | bytes 8000000 | tf_op jit(solution)/shard_map/pallas_call | solution.py:405
  44.4 3.6 %shard_map.69 = (bf16[1024,1024]{1,0:T(8,128)(2,1)}, bf16[128,1024]{1,0:T(8,128)(2,1)}) custom-call(s32[1,128]{1,0:T(1,128)} %bitcast.3, bf16[128,1024]{1,0:T(8,128)(2,1)} %x_hbm.3, bf16[1024,1024]{1,0:T(8,128)(2,1)} %rot_hbm.1, bf16[1024,1024]{1,0:T(8,128)(2,1)} %get-tuple-element.5.newc_from, bf16[16,16,512]{2,1,0:T(8,128)(2,1)} %get-tuple-element.6.rfb_from, ...), custom_call_target="tpu_custom_call" | custom-call | flops 400000000 | bytes 9000000 | tf_op jit(solution)/shard_map/pallas_call | solution.py:422
